TPU v7x, 32 devices: a whole 2x2x4 slice. The times are simulated.
32 devices in a mesh: depth: 4 (over x, core), lat: 8 (over z, y).
Axes of the slice: x: 2, y: 2, z: 4, core: 2. Of those that a mesh axis runs over, the one named last changes fastest.
Arguments:
- source_field: float32 [2, 4, 256, 1024], P(None, None, 'lat'), may hold values from -9 to 9, as said below
- receiver_field: float32 [2, 4, 256, 1024], P(None, None, 'lat'), may hold values from -9 to 9, as said below
- zone_index: int32 [16, 256, 1024], P('depth', 'lat'), may hold values from 0 to 2
- blend_weight: int32 [16, 256, 1024], P('depth', 'lat'), may hold values from 0 to 16
- ref_velocity: float32 [4], replicated, may hold values from 1500 to 4500
- frequencies: int32 [4], replicated, may hold values from 5 to 40
Outputs:
- migrated_image: float32 [16, 256, 1024], P('depth', 'lat')
Inputs may be any that keep to these rules, and one draw needn't show every extreme that they name: `source_field`: surface wavefields of order one. `receiver_field`: recorded wavefields of order one.
All inputs are finite; a program needn't handle non-finite values.
Results may differ from a plain program's by a relative error of at most 0.0003.
Values sent between devices are 32-bit elements; how exact they have to be, the bound alone decides.
No kernel may reach another device: no remote copies, remote signals or barrier semaphores. Data moves between devices by JAX's collectives and lax.ppermute only.
A program may use at most 64 MiB of HBM per device.

v0:
```python
import functools
import math

import jax
import jax.numpy as jnp
from jax import lax
from jax.experimental import pallas as pl
from jax.experimental.pallas import tpu as pltpu
from jax.sharding import PartitionSpec as P

HALF = 7
BLEND = 16
TAPS = 2 * HALF + 1
SPAN = 2 * HALF
LANES = 128
WIN = LANES - SPAN
BLK = 16
AXES = ("depth", "lat")
OFF = 8

cell_width = 5.0
depth_step = 10.0
taper_width = 16.0

f32 = jnp.float32
bf16 = jnp.bfloat16


def cdiv(a, b):
    return -(-a // b)


def kernels(frequencies, ref_velocity):
    offsets = jnp.arange(-HALF, HALF + 1, dtype=jnp.int32).astype(jnp.float32)
    wavenumber = 2.0 * math.pi * frequencies.astype(jnp.float32)[:, None] / ref_velocity[None, :]
    curvature = wavenumber * (cell_width * cell_width / (2.0 * depth_step))
    phase_turn = wavenumber * depth_step
    chirp_angle = curvature[:, :, None] * (offsets * offsets)[None, None, :]
    envelope = jnp.exp(-offsets * offsets / taper_width)
    raw_re = envelope * jnp.cos(chirp_angle)
    raw_im = envelope * jnp.sin(chirp_angle)
    magnitude = jnp.sqrt(jnp.sum(raw_re, axis=-1) ** 2 + jnp.sum(raw_im, axis=-1) ** 2)[:, :, None]
    return (raw_re / magnitude, raw_im / magnitude, jnp.cos(phase_turn), jnp.sin(phase_turn))


def operators(tap_re, tap_im, turn_cos, turn_sin):
    ph_re = tap_re * turn_cos[..., None] - tap_im * turn_sin[..., None]
    ph_im = tap_re * turn_sin[..., None] + tap_im * turn_cos[..., None]
    lines = jnp.stack([tap_re, tap_im, ph_re, ph_im], axis=2)
    return jnp.pad(lines, ((0, 0),) * 3 + ((0, LANES - TAPS),))


def split(v):
    high = v.astype(bf16)
    return high, (v - high.astype(f32)).astype(bf16)


def window(x, start, b):
    low = start + WIN * b
    high = min(low + LANES, x.shape[1])
    part = x[:, low:high]
    if high - low < LANES:
        part = jnp.concatenate(
            [part, jnp.zeros((x.shape[0], LANES - (high - low)), x.dtype)], axis=1
        )
    return part


def dense(get, start, count):
    pieces = []
    n = start
    while n < start + count:
        b = n // WIN
        end = min(WIN * (b + 1), start + count)
        pieces.append(get(b)[:, n - WIN * b : end - WIN * b])
        n = end
    return jnp.concatenate(pieces, axis=1)


CORE, HI, SIDE, EVEN_PAIR, FIRST_PAIR, LAST_PAIR, BLOCK, REL = range(8)


def edge_lanes(x, k, cols, n):
    none = jnp.zeros((x.shape[0], n), x.dtype)
    left = x[:, cols * k - n : cols * k] if k > 0 else none
    right = x[:, cols * (k + 1) : cols * (k + 1) + n] if k < 3 else none
    return left, right


def pack_tables_kernel(edge, info, zone, blend, keep, give):
    strip, width = zone.shape[1:]
    cols = width // 4
    half = zone.shape[0] // 2
    core = info[CORE]
    rest = jnp.zeros((strip, LANES - 4 * edge), jnp.int32)
    for k in range(4):
        slot = info[REL + k]
        for v in range(half):
            for ref, h in ((keep, core), (give, 1 - core)):
                z = zone[h * half + v] + OFF
                w = blend[h * half + v]
                zl, zr = edge_lanes(z, k, cols, edge)
                wl, wr = edge_lanes(w, k, cols, edge)
                ref[slot, v, :, 0:cols] = z[:, cols * k : cols * (k + 1)]
                ref[slot, v, :, cols : 2 * cols] = w[:, cols * k : cols * (k + 1)]
                ref[slot, v, :, 2 * cols : 2 * cols + LANES] = jnp.concatenate(
                    [zl, zr, wl, wr, rest], axis=1
                )


def pack_fields_kernel(halo, info, src, rcv, mine, send):
    per_core = mine.shape[0]
    strip, width = src.shape[2:]
    cols = width // 4
    rest = jnp.zeros((strip, LANES - 4 * halo), f32)
    for k in range(4):
        slot = info[REL + k]
        for place, ref in ((0, mine), (2, send)):

            @pl.when(slot == place)
            def _():
                for q in range(per_core):
                    at = info[CORE] * per_core + q
                    lefts, rights = [], []
                    for p in range(4):
                        x = (src if p < 2 else rcv)[p % 2, at]
                        if p == 3:
                            x = -x
                        ref[q, :, p * cols : (p + 1) * cols] = x[:, cols * k : cols * (k + 1)]
                        left, right = edge_lanes(x, k, cols, halo)
                        lefts.append(left)
                        rights.append(right)
                    ref[q, :, 4 * cols : 4 * cols + LANES] = jnp.concatenate(
                        lefts + [rest], axis=1
                    )
                    ref[q, :, 4 * cols + LANES : 4 * cols + 2 * LANES] = jnp.concatenate(
                        rights + [rest], axis=1
                    )


def operators_kernel(info, lines, rows_out, cols_out):
    count, refs = lines.shape[:2]
    lane = lax.broadcasted_iota(jnp.int32, (LANES, LANES), 1)
    for q in range(count):
        by_rows, by_cols = rows_out.at[q], cols_out.at[q]
        for j in range(refs):
            re, im, ph_re, ph_im = (lines[q, j, n : n + 1, :] for n in range(4))
            for p, line in enumerate(
                (re - pltpu.roll(im, 2 * BLK, 1), im + pltpu.roll(re, 2 * BLK, 1))
            ):
                x = pltpu.roll(
                    jnp.broadcast_to(line, (BLK, LANES)), 0, 1, stride=1, stride_axis=0
                )
                high, low = split(x)
                high, low = high[:, : 4 * BLK], low[:, : 4 * BLK]
                at = (2 * j + p) * BLK
                by_rows[at : at + BLK, :] = jnp.concatenate([high, high, low], axis=1)
            bands = []
            for line in (ph_re, ph_im):
                x = pltpu.roll(
                    jnp.broadcast_to(pltpu.roll(line, WIN, 1), (LANES, LANES)),
                    0,
                    1,
                    stride=1,
                    stride_axis=0,
                )
                bands.append(split(jnp.where(lane < WIN, x, 0.0)))
            for n, kind in enumerate((0, 0, 1)):
                x, y = bands[0][kind], bands[1][kind]
                at = 2 * LANES * n
                by_cols[j, at : at + LANES, 0:LANES] = x
                by_cols[j, at : at + LANES, LANES : 2 * LANES] = y
                by_cols[j, at + LANES : at + 2 * LANES, 0:LANES] = -y
                by_cols[j, at + LANES : at + 2 * LANES, LANES : 2 * LANES] = x


def edges_out(info, ref, send_a, send_b, count):
    size = ref.shape[-2]
    lead = (slice(None),) * (len(ref.shape) - 2)

    def put(top_to, bottom_to):
        top_to[lead + (slice(0, count),)] = ref[lead + (slice(0, count),)]
        bottom_to[lead + (slice(0, count),)] = ref[lead + (slice(size - count, size),)]

    pl.when(info[EVEN_PAIR] == 1)(lambda: put(send_b, send_a))
    pl.when(info[EVEN_PAIR] == 0)(lambda: put(send_a, send_b))


def join_tables_kernel(edge, sets, info, *refs):
    count = len(sets)
    whole, send_a, send_b, token = refs[4 * count :]
    token[...] = jnp.zeros_like(token)
    first = info[SIDE] == 0
    for n, s in enumerate(sets):
        mine, got_hi, got_side, got_both = refs[4 * n : 4 * n + 4]
        strip = mine.shape[1]
        near = jnp.where(info[HI] == s, mine[...], got_hi[...])
        far = jnp.where(info[HI] == s, got_side[...], got_both[...])
        whole[n, :, 0:strip, :] = jnp.where(first, near, far)
        whole[n, :, strip : 2 * strip, :] = jnp.where(first, far, near)
        edges_out(info, whole.at[n], send_a.at[n], send_b.at[n], edge)


def join_fields_kernel(halo, info, mine, got, whole, send_a, send_b, token):
    token[...] = jnp.zeros_like(token)
    strip = mine.shape[1]
    first = info[SIDE] == 0
    whole[:, 0:strip, :] = jnp.where(first, mine[...], got[...])
    whole[:, strip : 2 * strip, :] = jnp.where(first, got[...], mine[...])
    edges_out(info, whole, send_a, send_b, halo)


def columns_kernel(halo, info, mid, got_a, got_b, *refs):
    send_a, send_b, token = refs
    token[...] = jnp.zeros_like(token)
    even = info[EVEN_PAIR] == 1
    inner = info[BLOCK] % 2 == 0
    cols = mid.shape[2] // 4
    for q in range(mid.shape[0]):
        lefts, rights = [], []
        for p in range(4):
            for start, out in ((p * cols, lefts), ((p + 1) * cols - LANES, rights)):
                lanes = slice(start, start + LANES)
                a, b, m = got_a[q, :, lanes], got_b[q, :, lanes], mid[q, :, lanes]
                top = jnp.where(info[FIRST_PAIR] == 1, 0.0, jnp.where(even, b, a))
                bottom = jnp.where(info[LAST_PAIR] == 1, 0.0, jnp.where(even, a, b))
                rows = jnp.concatenate([top, m, bottom], axis=0)
                out.append(rows[:, :halo] if out is lefts else rows[:, LANES - halo :])
        rest = jnp.zeros((lefts[0].shape[0], LANES - 4 * halo), f32)
        left = jnp.concatenate(lefts + [rest], axis=1)
        right = jnp.concatenate(rights + [rest], axis=1)
        send_a[q] = jnp.where(inner, right, left)
        send_b[q] = jnp.where(inner, left, right)


def tables_kernel(
    cols, edge, windows, n, info, whole_m, whole_o, a_m, a_o, b_m, b_o, out
):
    whole_m, whole_o, a_m, a_o, b_m, b_o = (
        x.at[n] for x in (whole_m, whole_o, a_m, a_o, b_m, b_o)
    )
    half = whole_m.shape[0]
    levels, held = out.shape[:2]
    even = info[EVEN_PAIR] == 1
    for v in range(levels):
        own = info[CORE] == v // half
        i = v % half
        a = jnp.where(own, a_m[i], a_o[i])[:edge]
        b = jnp.where(own, b_m[i], b_o[i])[:edge]
        w = jnp.where(own, whole_m[i], whole_o[i])
        top = jnp.where(info[FIRST_PAIR] == 1, 0, jnp.where(even, b, a))
        bottom = jnp.where(info[LAST_PAIR] == 1, 0, jnp.where(even, a, b))
        x = jnp.concatenate([top, w, bottom], axis=0)
        s = 2 * cols
        z = jnp.concatenate([x[:, s : s + edge], x[:, :cols], x[:, s + edge : s + 2 * edge]], 1)
        s += 2 * edge
        w = jnp.concatenate(
            [x[:, s : s + edge], x[:, cols : 2 * cols], x[:, s + edge : s + 2 * edge]], 1
        )
        t = (z - OFF).astype(f32) + w.astype(f32) * (1.0 / BLEND)
        h = x.shape[0] - SPAN * v
        t = t[HALF * v : HALF * v + h]
        for b in range(windows):
            out[v, 0:h, b * LANES : (b + 1) * LANES] = window(t, HALF * v, b)
        out[v, h:held, :] = jnp.full((held - h, windows * LANES), -8.0, f32)


def stage_kernel(levels, halo, windows, blocks, refs, first, last, *args):
    args = list(args)
    info, token = args[:2]
    count = 3 if first else 5
    fields = args[2 : 2 + count]
    tw_ref, a_ref, c_ref = args[2 + count : 5 + count]
    img_ref = args[5 + count]
    outs = args[6 + count : 6 + count + (0 if last else 3)]
    scratch = args[6 + count + len(outs) :]

    def one(q, carry):
        stage_one(
            levels, halo, windows, blocks, refs, first, last, q,
            info, *(x.at[q] for x in fields), tw_ref, a_ref.at[q], c_ref.at[q], img_ref,
            *(x.at[q] for x in outs), *scratch,
        )
        return carry

    lax.fori_loop(0, fields[0].shape[0], one, 0)


def stage_one(levels, halo, windows, blocks, refs, first, last, freq, *args):
    args = list(args)
    info = args.pop(0)
    mid, got_a, got_b = args[:3]
    del args[:3]
    if not first:
        got_y, got_m = args[:2]
        del args[:2]
    tw_ref, a_ref, c_ref = args[:3]
    del args[:3]
    img_ref = args.pop(0)
    if not last:
        out_ref, send_a, send_b = args[:3]
        del args[:3]
    cur_ref, y_ref, im_ref = args
    rows = mid.shape[0]
    cols = img_ref.shape[2]
    height = rows + 2 * halo
    held = cur_ref.shape[2]
    each = 2 * windows
    lanes = windows * LANES

    even = info[EVEN_PAIR] == 1
    inner = info[BLOCK] % 2 == 0

    def rows_of(lane):
        a, b = got_a[:, lane], got_b[:, lane]
        top = jnp.where(info[FIRST_PAIR] == 1, 0.0, jnp.where(even, b, a))
        bottom = jnp.where(info[LAST_PAIR] == 1, 0.0, jnp.where(even, a, b))
        return jnp.concatenate([top, mid[:, lane], bottom], axis=0)

    if first:
        left = rows_of(slice(4 * cols, 4 * cols + LANES))
        right = rows_of(slice(4 * cols + LANES, 4 * cols + 2 * LANES))
    else:
        left = jnp.where(info[BLOCK] == 0, 0.0, jnp.where(inner, got_m[...], got_y[...]))
        right = jnp.where(info[BLOCK] == 3, 0.0, jnp.where(inner, got_y[...], got_m[...]))
    for f in range(2):
        for p in range(2):
            n = 2 * f + p
            x = jnp.concatenate(
                [
                    left[:, n * halo : (n + 1) * halo],
                    rows_of(slice(n * cols, (n + 1) * cols)),
                    right[:, n * halo : (n + 1) * halo],
                ],
                axis=1,
            )
            for b in range(windows):
                high, low = split(window(x, 0, b))
                at = (f * windows + b) * LANES
                cur_ref[p, 0, 0:height, at : at + LANES] = high
                cur_ref[p, 1, 0:height, at : at + LANES] = low
    if held > height:
        cur_ref[:, :, height:held, :] = jnp.zeros((2, 2, held - height, 2 * lanes), bf16)
    lane = lax.broadcasted_iota(jnp.int32, (BLK, LANES), 1)

    def chunk(l, base, blocks):
        for k in range(blocks):
            r = pl.ds(base + BLK * k, 2 * BLK)
            rhi, rlo = cur_ref[0, 0, r, :], cur_ref[0, 1, r, :]
            ihi, ilo = cur_ref[1, 0, r, :], cur_ref[1, 1, r, :]
            rhs = jnp.concatenate([rhi, ihi, rlo, ilo, rhi, ihi], axis=0)
            g = jnp.dot(a_ref[...], rhs, preferred_element_type=f32)
            high, low = split(g)
            for j in range(refs):
                for p in range(2):
                    s = (2 * j + p) * BLK
                    for q in range(each):
                        rr = (k * each + q) * BLK
                        at = q * LANES
                        y_ref[j, rr : rr + BLK, p * LANES : (p + 1) * LANES] = high[
                            s : s + BLK, at : at + LANES
                        ]
                        y_ref[j, rr : rr + BLK, (2 + p) * LANES : (3 + p) * LANES] = low[
                            s : s + BLK, at : at + LANES
                        ]
        t = tw_ref[l, pl.ds(base, BLK * blocks), :]
        acc = None
        for j in range(refs):
            y = y_ref[j, : blocks * each * BLK]
            full = jnp.dot(
                jnp.concatenate([y, y[:, : 2 * LANES]], axis=1),
                c_ref[j],
                preferred_element_type=f32,
            )
            w = jnp.maximum(1.0 - jnp.abs(t - float(j)), 0.0)
            new = []
            for k in range(blocks):
                for f in range(2):
                    for b in range(windows):
                        rr = (k * each + f * windows + b) * BLK
                        wk = w[BLK * k : BLK * (k + 1), b * LANES : (b + 1) * LANES]
                        new.append(
                            (wk * full[rr : rr + BLK, :LANES], wk * full[rr : rr + BLK, LANES:])
                        )
            if acc is None:
                acc = new
            else:
                acc = [(a0 + b0, a1 + b1) for (a0, a1), (b0, b1) in zip(acc, new)]
        for k in range(blocks):
            r = pl.ds(base + BLK * k, BLK)
            for b in range(windows):
                s = acc[k * each + b]
                q = acc[k * each + windows + b]
                im_ref[l, r, b * LANES : (b + 1) * LANES] = s[0] * q[0] - s[1] * q[1]
            for f in range(2):
                for b in range(windows):
                    at = (f * windows + b) * LANES
                    for p in range(2):
                        v = acc[k * each + f * windows + b][p]
                        if b + 1 < windows:
                            after = pltpu.roll(acc[k * each + f * windows + b + 1][p], WIN, 1)
                            v = jnp.where(lane < WIN, v, after)
                        high, low = split(v)
                        cur_ref[p, 0, r, at : at + LANES] = high
                        cur_ref[p, 1, r, at : at + LANES] = low

    for l in range(levels):
        need = cdiv(height - SPAN * (l + 1), BLK)
        parts = cdiv(need, blocks)
        at = 0
        for i in range(parts):
            n = cdiv(need - at, parts - i)
            chunk(l, at * BLK, n)
            at += n
    if not last:
        for f in range(2):
            for p in range(2):

                def get(b):
                    at = (f * windows + b) * LANES
                    return cur_ref[p, 0, 0:rows, at : at + LANES].astype(f32) + cur_ref[
                        p, 1, 0:rows, at : at + LANES
                    ].astype(f32)

                n = 2 * f + p
                out_ref[:, n * cols : (n + 1) * cols] = dense(get, 0, cols)
        edges_out(info, out_ref, send_a, send_b, halo)
    for l in range(levels):
        o = HALF * (levels - 1 - l)
        part = dense(
            lambda b: im_ref[l, o : o + rows, b * LANES : (b + 1) * LANES], o, cols
        )
        img_ref[l] = jnp.where(freq == 0, part, img_ref[l] + part)


def call(body, out_shape, info, *args, after=(), hand=(), **more):
    near = [pl.BlockSpec(memory_space=pltpu.VMEM)] * len(args)
    far = [pl.BlockSpec(memory_space=pl.ANY)]
    count = 1 + len(args)
    skip = count + len(after) + 2 * len(hand)

    def run(*refs):
        body(*refs[:count], *refs[skip:])

    out_specs = jax.tree.map(lambda _: pl.BlockSpec(memory_space=pltpu.VMEM), out_shape)
    if hand:
        out_shape = [shape(*x.shape, dtype=x.dtype) for x in hand] + out_shape
        out_specs = far * len(hand) + out_specs
        first = count + len(after)
        more["input_output_aliases"] = {first + n: n for n in range(len(hand))}
    return pl.pallas_call(
        run,
        in_specs=[pl.BlockSpec(memory_space=pltpu.SMEM)] + near + far * (len(after) + len(hand)),
        out_specs=out_specs,
        out_shape=out_shape,
        compiler_params=pltpu.CompilerParams(vmem_limit_bytes=40 * 2**20),
        **more,
    )(info, *args, *after, *hand)


def shape(*dims, dtype=f32):
    return jax.ShapeDtypeStruct(dims, dtype)


def local(source_field, receiver_field, zone_index, blend_weight, ref_velocity, frequencies):
    depth, lat = lax.axis_size("depth"), lax.axis_size("lat")
    d, l = lax.axis_index("depth"), lax.axis_index("lat")
    hi, core = d // 2, d % 2
    pair, side = l // 2, l % 2
    if depth != 4 or lat % 4:
        raise ValueError("mesh")
    levels, strip, width = zone_index.shape
    freq_count, refs = frequencies.shape[0], ref_velocity.shape[0]
    per_core = freq_count // 2
    rows, cols = 2 * strip, width // 4
    halo = HALF * levels
    edge = halo - HALF
    half = levels // 2
    windows = cdiv(cols + SPAN * (levels - 1), WIN)
    blocks = cdiv(rows + 2 * halo - SPAN, BLK)
    held = cdiv(rows + 2 * halo - SPAN, BLK) * BLK + BLK

    def permutation(move):
        out = []
        for i in range(depth * lat):
            dd, ll = divmod(i, lat)
            h, c, p, s = dd // 2, dd % 2, ll // 2, ll % 2
            target = move(h, c, p, s)
            if target is None or not 0 <= target[2] < lat // 2:
                target = (h, 1 - c, p, s)
            h, c, p, s = target
            out.append((i, (h * 2 + c) * lat + p * 2 + s))
        return out

    across_hi = permutation(lambda h, c, p, s: (1 - h, c, p, s))
    across_side = permutation(lambda h, c, p, s: (h, c, p, 1 - s))
    across_both = permutation(lambda h, c, p, s: (1 - h, c, p, 1 - s))
    across_core = permutation(lambda h, c, p, s: (h, 1 - c, p, s))
    pairs_even = permutation(lambda h, c, p, s: (h, c, p + 1 - 2 * (p % 2), s))
    pairs_odd = permutation(lambda h, c, p, s: (h, c, p - 1 + 2 * (p % 2), s))
    middle = permutation(lambda h, c, p, s: (1 - h, c, p, s) if s == 1 else None)

    def move(x, pairs):
        return lax.ppermute(x, AXES, pairs)

    def place(h, s):
        return 2 * h + jnp.where(h == 0, s, 1 - s)

    block = place(hi, side)
    rel = []
    for k in range(4):
        kh = k // 2
        ks = k % 2 if kh == 0 else 1 - k % 2
        rel.append(jnp.where(hi == kh, 0, 1) + jnp.where(side == ks, 0, 2))
    info = jnp.stack(
        [
            core,
            hi,
            side,
            (pair % 2 == 0).astype(jnp.int32),
            (pair == 0).astype(jnp.int32),
            (pair == lat // 2 - 1).astype(jnp.int32),
            block,
        ]
        + rel
    ).astype(jnp.int32)

    mark = shape(8, LANES)
    lane_t = 2 * cols + LANES
    lane_f = 4 * cols + 2 * LANES
    packed = shape(4, half, strip, lane_t, dtype=jnp.int32)
    keep, give = call(
        functools.partial(pack_tables_kernel, edge),
        [packed, packed],
        info,
        zone_index,
        blend_weight,
    )
    swapped = move(give, across_core)

    mine, send = call(
        functools.partial(pack_fields_kernel, halo),
        [shape(per_core, strip, lane_f)] * 2,
        info,
        source_field,
        receiver_field,
        after=[give],
    )
    got = move(send, across_side)

    def spread(own):
        return (
            own[0],
            move(own[1], across_hi),
            move(own[2], across_side),
            move(own[3], across_both),
        )

    def join(sets, parts, after):
        edges = shape(len(sets), half, cdiv(edge, 8) * 8, lane_t, dtype=jnp.int32)
        whole, send_a, send_b, token = call(
            functools.partial(join_tables_kernel, edge, sets),
            [shape(len(sets), half, rows, lane_t, dtype=jnp.int32), edges, edges, mark],
            info,
            *parts,
            after=after,
        )
        return (
            whole,
            move(whole, across_core),
            move(send_a, pairs_even),
            move(send_b, pairs_odd),
            token,
        )

    def finish(whole, other, got_a, got_b):
        swap_a, swap_b = move(got_a, across_core), move(got_b, across_core)
        return [
            call(
                functools.partial(tables_kernel, cols, edge, windows, n),
                shape(levels, held, windows * LANES),
                info,
                whole,
                other,
                got_a,
                swap_a,
                got_b,
                swap_b,
            )
            for n in range(whole.shape[0])
        ]

    parts = [spread(jnp.where(core == 0, keep, swapped)), None]

    taps = kernels(frequencies, ref_velocity)
    taps = [lax.dynamic_slice_in_dim(x, core * per_core, per_core, 0) for x in taps]
    matrices = call(
        operators_kernel,
        [
            shape(per_core, refs * 2 * BLK, 12 * BLK, dtype=bf16),
            shape(per_core, refs, 6 * LANES, 2 * LANES, dtype=bf16),
        ],
        info,
        operators(*taps),
        after=[give],
    )

    *joined, token = join((0,), parts[0], [matrices[0]])
    tables = finish(*joined)
    parts[1] = spread(jnp.where(core == 1, keep, swapped))
    whole, send_a, send_b, token = call(
        functools.partial(join_fields_kernel, halo),
        [shape(per_core, rows, lane_f)] + [shape(per_core, halo, lane_f)] * 2 + [mark],
        info,
        mine,
        got,
        after=[joined[0]],
    )
    state = (whole, move(send_a, pairs_even), move(send_b, pairs_odd))

    area = levels * (rows + halo) * windows * LANES
    images = []
    for s in range(4):
        out_shape = [shape(levels, rows, cols)]
        if s < 3:
            out_shape += [shape(per_core, rows, 4 * cols)] + [shape(per_core, halo, 4 * cols)] * 2
        image, *fields = call(
            functools.partial(
                stage_kernel, levels, halo, windows, blocks, refs, s == 0, s == 3
            ),
            out_shape,
            info,
            token,
            *state,
            tables[s],
            *matrices,
            scratch_shapes=[
                pltpu.VMEM((2, 2, held, 2 * windows * LANES), bf16),
                pltpu.VMEM((refs, blocks * 2 * windows * BLK, 4 * LANES), bf16),
                pltpu.VMEM((levels, held, windows * LANES), f32),
            ],
            cost_estimate=pl.CostEstimate(
                flops=area * 8 * refs * 2 * 3 * 512, bytes_accessed=2**21, transcendentals=0
            ),
        )
        images.append(image)
        if s == 3:
            break
        if s == 0:
            *joined, _ = join((0,), parts[1], [image])
        field, send_a, send_b = fields
        got = [move(send_a, pairs_even), move(send_b, pairs_odd)]
        *handed, side_a, side_b, token = call(
            functools.partial(columns_kernel, halo),
            [shape(per_core, rows + 2 * halo, LANES)] * 2 + [mark],
            info,
            field,
            *got,
            hand=list(joined[2:]) if s < 2 else [],
        )
        state = (field, *got, move(side_a, across_side), move(side_b, middle))
        if s < 2:
            tables += finish(*joined[:2], *handed)
        if s == 0:
            *joined, token = join((1, 1), parts[0] + parts[1], [token])

    sums = [x + move(x, across_core) for x in images]
    sets = [jnp.where(core == 0, sums[2 * s], sums[2 * s + 1]) for s in range(2)]
    here = jnp.where(hi == 0, sets[0], sets[1])
    there = jnp.where(hi == 0, sets[1], sets[0])

    def strip_of(x, s):
        return lax.dynamic_slice_in_dim(x, s * strip, strip, 1)

    mine = strip_of(here, side)
    got_hi = move(strip_of(there, side), across_hi)
    got_side = move(strip_of(here, 1 - side), across_side)
    got_both = move(strip_of(there, 1 - side), across_both)
    pieces = []
    for k in range(4):
        piece = jnp.where(
            block == k,
            mine,
            jnp.where(
                place(1 - hi, side) == k,
                got_hi,
                jnp.where(place(hi, 1 - side) == k, got_side, got_both),
            ),
        )
        pieces.append(piece)
    return jnp.concatenate(pieces, axis=2) * (1.0 / freq_count)


def solution(mesh):
    in_specs = (
        P(None, None, "lat", None),
        P(None, None, "lat", None),
        P("depth", "lat", None),
        P("depth", "lat", None),
        P(),
        P(),
    )
    out_specs = P("depth", "lat", None)
    return jax.shard_map(local, mesh=mesh, in_specs=in_specs, out_specs=out_specs, check_vma=False)
```

profile of v0, /device:TPU:0, one launch (start us, length us, event | category | flops | bytes accessed | tf_op | source)
XLA Modules:
  0.0 154.5 jit_solution(16117434074762969706)
XLA Ops:
  6.8 2.6 %collective-permute-start = (f32[2,32,1280]{2,1,0:T(8,128)S(1)}, f32[2,32,1280]{2,1,0:T(8,128)S(1)}, u32[]{:S(2)}, u32[]{:S(2)}) collective-permute-start(f32[2,32,1280]{2,1,0:T(8,128)S(1)} %get-tuple-element.52), channel_id=1, source_target_pairs={{0,1},{1,0},{2,3},{3,2},{4,5},{5,4},{6,7},{7,6},{8,9},{9,8},{10,11... | collective-permute-start | bytes 983048 | tf_op jit(solution)/shard_map/ppermute | solution.py:504
  10.1 1.6 %collective-permute-start.2 = (s32[2,32,640]{2,1,0:T(8,128)S(1)}, s32[2,32,640]{2,1,0:T(8,128)S(1)}, u32[]{:S(2)}, u32[]{:S(2)}) collective-permute-start(s32[2,32,640]{2,1,0:T(8,128)S(1)} %get-tuple-element.115), channel_id=1, source_target_pairs={{0,16},{1,17},{2,18},{3,19},{4,20},{5,21},{6,22},{7,23},{8,24},{9,... | collective-permute-start | bytes 491528 | tf_op jit(solution)/shard_map/ppermute | solution.py:504
  12.2 1.5 collective-permute-start.4
  13.8 2.2 %shard_map.66 = (bf16[2,128,192]{2,1,0:T(8,128)(2,1)S(1)}, bf16[2,4,768,256]{3,2,1,0:T(8,128)(2,1)S(1)}) custom-call(s32[11]{0:T(128)S(1)} %stack.74.refs_0_, f32[2,4,4,128]{3,2,1,0:T(4,128)S(1)} %select_maximum_fusion.refs_1_, s32[4,2,32,640]{3,2,1,0:T(8,128)S(1)} %get-tuple-element.50.refs_3_.refs_2_), custom_call_target="tpu_custom_call" | custom-call | tf_op jit(solution)/shard_map/pallas_call | solution.py:451
  17.2 7.6 %collective-permute-done.3.refs_3_ = s32[2,32,640]{2,1,0:T(8,128)S(1)} collective-permute-done((s32[2,32,640]{2,1,0:T(8,128)S(1)}, s32[2,32,640]{2,1,0:T(8,128)S(1)}, u32[]{:S(2)}, u32[]{:S(2)}) %collective-permute-start.3) | collective-permute-done | bytes 163872 | tf_op jit(solution)/shard_map/ppermute | solution.py:504
  26.0 3.4 %collective-permute-start.8 = (s32[1,2,24,640]{3,2,1,0:T(8,128)S(1)}, s32[1,2,24,640]{3,2,1,0:T(8,128)S(1)}, u32[]{:S(2)}, u32[]{:S(2)}) collective-permute-start(s32[1,2,24,640]{3,2,1,0:T(8,128)S(1)} %get-tuple-element.60), channel_id=1, source_target_pairs={{0,2},{1,3},{2,0},{3,1},{4,6},{5,7},{6,4},{7,5},{8,10},{9,11},{10,... | collective-permute-start | bytes 368648 | tf_op jit(solution)/shard_map/ppermute | solution.py:504
  30.8 1.8 %collective-permute-done.8.refs_3_ = s32[1,2,24,640]{3,2,1,0:T(8,128)S(1)} collective-permute-done((s32[1,2,24,640]{3,2,1,0:T(8,128)S(1)}, s32[1,2,24,640]{3,2,1,0:T(8,128)S(1)}, u32[]{:S(2)}, u32[]{:S(2)}) %collective-permute-start.8) | collective-permute-done | bytes 122912 | tf_op jit(solution)/shard_map/ppermute | solution.py:504
  32.7 1.6 %collective-permute-start.13 = (s32[2,32,640]{2,1,0:T(8,128)S(1)}, s32[2,32,640]{2,1,0:T(8,128)S(1)}, u32[]{:S(2)}, u32[]{:S(2)}) collective-permute-start(s32[2,32,640]{2,1,0:T(8,128)S(1)} %get-tuple-element.111), channel_id=1, source_target_pairs={{0,16},{1,17},{2,18},{3,19},{4,20},{5,21},{6,22},{7,23},{8,24},{9,... | collective-permute-start | bytes 491528 | tf_op jit(solution)/shard_map/ppermute | solution.py:504
  34.2 1.5 collective-permute-start.14
  36.9 1.3 shard_map.69.refs_5_
  38.2 2.0 %collective-permute-done.5.refs_3_ = f32[2,28,1280]{2,1,0:T(8,128)S(1)} collective-permute-done((f32[2,28,1280]{2,1,0:T(8,128)S(1)}, f32[2,28,1280]{2,1,0:T(8,128)S(1)}, u32[]{:S(2)}, u32[]{:S(2)}) %collective-permute-start.5) | collective-permute-done | bytes 286752 | tf_op jit(solution)/shard_map/ppermute | solution.py:504
  40.2 13.3 %shard_map.70 = (f32[4,64,256]{2,1,0:T(8,128)S(1)}, f32[2,64,1024]{2,1,0:T(8,128)S(1)}, f32[2,28,1024]{2,1,0:T(8,128)S(1)}, f32[2,28,1024]{2,1,0:T(8,128)S(1)}) custom-call(s32[11]{0:T(128)S(1)} %stack.74.refs_0_, f32[8,128]{1,0:T(8,128)S(1)} %get-tuple-element.56.refs_1_, f32[2,64,1280]{2,1,0:T(8,128)S(1)} %get-tuple-element.57.refs_2_, ...), custom_call_target="tpu_custom_call" | custom-call | flops 13891534848 | bytes 2097152 | tf_op jit(solution)/shard_map/pallas_call | solution.py:451
  53.5 1.8 %collective-permute-start.16 = (f32[2,28,1024]{2,1,0:T(8,128)S(1)}, f32[2,28,1024]{2,1,0:T(8,128)S(1)}, u32[]{:S(2)}, u32[]{:S(2)}) collective-permute-start(f32[2,28,1024]{2,1,0:T(8,128)S(1)} %get-tuple-element.65), channel_id=1, source_target_pairs={{0,2},{1,3},{2,0},{3,1},{4,6},{5,7},{6,4},{7,5},{8,10},{9,11},{10,... | collective-permute-start | bytes 688136 | tf_op jit(solution)/shard_map/ppermute | solution.py:504
  58.6 5.6 %collective-permute-done.18.refs_4_ = s32[1,2,24,640]{3,2,1,0:T(8,128)S(1)} collective-permute-done((s32[1,2,24,640]{3,2,1,0:T(8,128)S(1)}, s32[1,2,24,640]{3,2,1,0:T(8,128)S(1)}, u32[]{:S(2)}, u32[]{:S(2)}) %collective-permute-start.18) | collective-permute-done | bytes 122912 | tf_op jit(solution)/shard_map/ppermute | solution.py:504
  65.6 1.5 collective-permute-start.20
  67.8 1.8 %collective-permute-start.28 = (s32[2,2,24,640]{3,2,1,0:T(8,128)S(1)}, s32[2,2,24,640]{3,2,1,0:T(8,128)S(1)}, u32[]{:S(2)}, u32[]{:S(2)}) collective-permute-start(s32[2,2,24,640]{3,2,1,0:T(8,128)S(1)} %get-tuple-element.80), channel_id=1, source_target_pairs={{0,2},{1,3},{2,0},{3,1},{4,6},{5,7},{6,4},{7,5},{8,10},{9,11},{10,... | collective-permute-start | bytes 737288 | tf_op jit(solution)/shard_map/ppermute | solution.py:504
  70.1 1.3 shard_map.74.refs_7_
  71.5 13.5 %shard_map.75 = (f32[4,64,256]{2,1,0:T(8,128)S(1)}, f32[2,64,1024]{2,1,0:T(8,128)S(1)}, f32[2,28,1024]{2,1,0:T(8,128)S(1)}, f32[2,28,1024]{2,1,0:T(8,128)S(1)}) custom-call(s32[11]{0:T(128)S(1)} %stack.74.refs_0_, f32[8,128]{1,0:T(8,128)S(1)} %get-tuple-element.70.refs_1_, f32[2,64,1024]{2,1,0:T(8,128)S(1)} %get-tuple-element.64.refs_1_.refs_2_, ...), custom_call_target="tpu_custom_call" | custom-call | flops 13891534848 | bytes 2097152 | tf_op jit(solution)/shard_map/pallas_call | solution.py:451
  85.0 1.4 collective-permute-start.26
  86.6 6.9 %collective-permute-done.26.refs_2_.refs_3_ = f32[2,28,1024]{2,1,0:T(8,128)S(1)} collective-permute-done((f32[2,28,1024]{2,1,0:T(8,128)S(1)}, f32[2,28,1024]{2,1,0:T(8,128)S(1)}, u32[]{:S(2)}, u32[]{:S(2)}) %collective-permute-start.26) | collective-permute-done | bytes 229408 | tf_op jit(solution)/shard_map/ppermute | solution.py:504
  94.9 1.8 %collective-permute-start.30 = (f32[2,120,128]{2,1,0:T(8,128)S(1)}, f32[2,120,128]{2,1,0:T(8,128)S(1)}, u32[]{:S(2)}, u32[]{:S(2)}) collective-permute-start(f32[2,120,128]{2,1,0:T(8,128)S(1)} %get-tuple-element.83), channel_id=1, source_target_pairs={{0,1},{1,0},{2,3},{3,2},{4,5},{5,4},{6,7},{7,6},{8,9},{9,8},{10,11... | collective-permute-start | bytes 368648 | tf_op jit(solution)/shard_map/ppermute | solution.py:504
  98.1 2.2 %collective-permute-done.30.refs_5_ = f32[2,120,128]{2,1,0:T(8,128)S(1)} collective-permute-done((f32[2,120,128]{2,1,0:T(8,128)S(1)}, f32[2,120,128]{2,1,0:T(8,128)S(1)}, u32[]{:S(2)}, u32[]{:S(2)}) %collective-permute-start.30) | collective-permute-done | bytes 122912 | tf_op jit(solution)/shard_map/ppermute | solution.py:504
  100.3 13.5 %shard_map.78 = (f32[4,64,256]{2,1,0:T(8,128)S(1)}, f32[2,64,1024]{2,1,0:T(8,128)S(1)}, f32[2,28,1024]{2,1,0:T(8,128)S(1)}, f32[2,28,1024]{2,1,0:T(8,128)S(1)}) custom-call(s32[11]{0:T(128)S(1)} %stack.74.refs_0_, f32[8,128]{1,0:T(8,128)S(1)} %get-tuple-element.82.refs_1_, f32[2,64,1024]{2,1,0:T(8,128)S(1)} %get-tuple-element.77.refs_1_.refs_2_, ...), custom_call_target="tpu_custom_call" | custom-call | flops 13891534848 | bytes 2097152 | tf_op jit(solution)/shard_map/pallas_call | solution.py:451
  113.8 1.9 %collective-permute-start.36 = (f32[2,28,1024]{2,1,0:T(8,128)S(1)}, f32[2,28,1024]{2,1,0:T(8,128)S(1)}, u32[]{:S(2)}, u32[]{:S(2)}) collective-permute-start(f32[2,28,1024]{2,1,0:T(8,128)S(1)} %get-tuple-element.90), channel_id=1, source_target_pairs={{0,2},{1,3},{2,0},{3,1},{4,6},{5,7},{6,4},{7,5},{8,10},{9,11},{10,... | collective-permute-start | bytes 688136 | tf_op jit(solution)/shard_map/ppermute | solution.py:504
  115.7 5.9 %collective-permute-done.36.refs_2_.refs_3_ = f32[2,28,1024]{2,1,0:T(8,128)S(1)} collective-permute-done((f32[2,28,1024]{2,1,0:T(8,128)S(1)}, f32[2,28,1024]{2,1,0:T(8,128)S(1)}, u32[]{:S(2)}, u32[]{:S(2)}) %collective-permute-start.36) | collective-permute-done | bytes 229408 | tf_op jit(solution)/shard_map/ppermute | solution.py:504
  122.5 1.6 %collective-permute-start.38 = (f32[2,120,128]{2,1,0:T(8,128)S(1)}, f32[2,120,128]{2,1,0:T(8,128)S(1)}, u32[]{:S(2)}, u32[]{:S(2)}) collective-permute-start(f32[2,120,128]{2,1,0:T(8,128)S(1)} %get-tuple-element.93), channel_id=1, source_target_pairs={{0,1},{1,0},{2,3},{3,2},{4,5},{5,4},{6,7},{7,6},{8,9},{9,8},{10,11... | collective-permute-start | bytes 368648 | tf_op jit(solution)/shard_map/ppermute | solution.py:504
  127.4 12.9 %shard_map.81 = f32[4,64,256]{2,1,0:T(8,128)S(1)} custom-call(s32[11]{0:T(128)S(1)} %stack.74.refs_0_, f32[8,128]{1,0:T(8,128)S(1)} %get-tuple-element.92.refs_1_, f32[2,64,1024]{2,1,0:T(8,128)S(1)} %get-tuple-element.89.refs_1_.refs_2_, f32[2,28,1024]{2,1,0:T(8,128)S(1)} %collective-permute-done.36.refs_2_.refs_3_, ...), custom_call_target="tpu_custom_call" | custom-call | flops 13891534848 | bytes 2097152 | tf_op jit(solution)/shard_map/pallas_call | solution.py:451
  140.4 1.5 collective-permute-done.40
  143.4 2.3 %collective-permute-start.43 = (f32[4,32,256]{2,1,0:T(8,128)S(1)}, f32[4,32,256]{2,1,0:T(8,128)S(1)}, u32[]{:S(2)}, u32[]{:S(2)}) collective-permute-start(f32[4,32,256]{2,1,0:T(8,128)S(1)} %get-tuple-element.117), channel_id=1, source_target_pairs={{0,17},{1,16},{2,19},{3,18},{4,21},{5,20},{6,23},{7,22},{8,25},{9,... | collective-permute-start | bytes 393224 | tf_op jit(solution)/shard_map/ppermute | solution.py:504
  145.8 2.3 %collective-permute-done.41 = f32[4,32,256]{2,1,0:T(8,128)S(1)} collective-permute-done((f32[4,32,256]{2,1,0:T(8,128)S(1)}, f32[4,32,256]{2,1,0:T(8,128)S(1)}, u32[]{:S(2)}, u32[]{:S(2)}) %collective-permute-start.41) | collective-permute-done | bytes 131104 | tf_op jit(solution)/shard_map/ppermute | solution.py:504
  148.2 4.0 %collective-permute-done.43 = f32[4,32,256]{2,1,0:T(8,128)S(1)} collective-permute-done((f32[4,32,256]{2,1,0:T(8,128)S(1)}, f32[4,32,256]{2,1,0:T(8,128)S(1)}, u32[]{:S(2)}, u32[]{:S(2)}) %collective-permute-start.43) | collective-permute-done | bytes 131104 | tf_op jit(solution)/shard_map/ppermute | solution.py:504
  152.1 1.4 collective-permute-done.42
  (106 shorter events, 28.4 us)
Async XLA Ops:
  3.0 6.9 %collective-permute-start.1 = (s32[4,2,32,640]{3,2,1,0:T(8,128)S(1)}, s32[4,2,32,640]{3,2,1,0:T(8,128)S(1)}, u32[]{:S(2)}, u32[]{:S(2)}) collective-permute-start(s32[4,2,32,640]{3,2,1,0:T(8,128)S(1)} %get-tuple-element.50.refs_3_.refs_2_), channel_id=1, source_target_pairs={{0,8},{1,9},{2,10},{3,11},{4,12},{5,13},{6,14},{7,15},{8,0},{9,1},... | collective-permute-start | bytes 1966088 | tf_op jit(solution)/shard_map/ppermute | solution.py:504
  6.8 22.6 %collective-permute-start = (f32[2,32,1280]{2,1,0:T(8,128)S(1)}, f32[2,32,1280]{2,1,0:T(8,128)S(1)}, u32[]{:S(2)}, u32[]{:S(2)}) collective-permute-start(f32[2,32,1280]{2,1,0:T(8,128)S(1)} %get-tuple-element.52), channel_id=1, source_target_pairs={{0,1},{1,0},{2,3},{3,2},{4,5},{5,4},{6,7},{7,6},{8,9},{9,8},{10,11... | collective-permute-start | bytes 983048 | tf_op jit(solution)/shard_map/ppermute | solution.py:504
  10.1 7.1 %collective-permute-start.2 = (s32[2,32,640]{2,1,0:T(8,128)S(1)}, s32[2,32,640]{2,1,0:T(8,128)S(1)}, u32[]{:S(2)}, u32[]{:S(2)}) collective-permute-start(s32[2,32,640]{2,1,0:T(8,128)S(1)} %get-tuple-element.115), channel_id=1, source_target_pairs={{0,16},{1,17},{2,18},{3,19},{4,20},{5,21},{6,22},{7,23},{8,24},{9,... | collective-permute-start | bytes 491528 | tf_op jit(solution)/shard_map/ppermute | solution.py:504
  11.7 13.1 %collective-permute-start.3 = (s32[2,32,640]{2,1,0:T(8,128)S(1)}, s32[2,32,640]{2,1,0:T(8,128)S(1)}, u32[]{:S(2)}, u32[]{:S(2)}) collective-permute-start(s32[2,32,640]{2,1,0:T(8,128)S(1)} %get-tuple-element.114), channel_id=1, source_target_pairs={{0,1},{1,0},{2,3},{3,2},{4,5},{5,4},{6,7},{7,6},{8,9},{9,8},{10,11... | collective-permute-start | bytes 491528 | tf_op jit(solution)/shard_map/ppermute | solution.py:504
  12.2 12.6 %collective-permute-start.4 = (s32[2,32,640]{2,1,0:T(8,128)S(1)}, s32[2,32,640]{2,1,0:T(8,128)S(1)}, u32[]{:S(2)}, u32[]{:S(2)}) collective-permute-start(s32[2,32,640]{2,1,0:T(8,128)S(1)} %get-tuple-element.113), channel_id=1, source_target_pairs={{0,17},{1,16},{2,19},{3,18},{4,21},{5,20},{6,23},{7,22},{8,25},{9,... | collective-permute-start | bytes 491528 | tf_op jit(solution)/shard_map/ppermute | solution.py:504
  26.0 6.6 %collective-permute-start.8 = (s32[1,2,24,640]{3,2,1,0:T(8,128)S(1)}, s32[1,2,24,640]{3,2,1,0:T(8,128)S(1)}, u32[]{:S(2)}, u32[]{:S(2)}) collective-permute-start(s32[1,2,24,640]{3,2,1,0:T(8,128)S(1)} %get-tuple-element.60), channel_id=1, source_target_pairs={{0,2},{1,3},{2,0},{3,1},{4,6},{5,7},{6,4},{7,5},{8,10},{9,11},{10,... | collective-permute-start | bytes 368648 | tf_op jit(solution)/shard_map/ppermute | solution.py:504
  29.4 6.4 %collective-permute-start.7 = (s32[1,2,64,640]{3,2,1,0:T(8,128)S(1)}, s32[1,2,64,640]{3,2,1,0:T(8,128)S(1)}, u32[]{:S(2)}, u32[]{:S(2)}) collective-permute-start(s32[1,2,64,640]{3,2,1,0:T(8,128)S(1)} %get-tuple-element.55.refs_3_.refs_1_), channel_id=1, source_target_pairs={{0,8},{1,9},{2,10},{3,11},{4,12},{5,13},{6,14},{7,15},{8,0},{9,1},... | collective-permute-start | bytes 983048 | tf_op jit(solution)/shard_map/ppermute | solution.py:504
  30.0 10.2 %collective-permute-start.5 = (f32[2,28,1280]{2,1,0:T(8,128)S(1)}, f32[2,28,1280]{2,1,0:T(8,128)S(1)}, u32[]{:S(2)}, u32[]{:S(2)}) collective-permute-start(f32[2,28,1280]{2,1,0:T(8,128)S(1)} %get-tuple-element.58), channel_id=1, source_target_pairs={{0,2},{1,3},{2,0},{3,1},{4,6},{5,7},{6,4},{7,5},{8,10},{9,11},{10,... | collective-permute-start | bytes 860168 | tf_op jit(solution)/shard_map/ppermute | solution.py:504
  30.1 10.1 %collective-permute-start.6 = (f32[2,28,1280]{2,1,0:T(8,128)S(1)}, f32[2,28,1280]{2,1,0:T(8,128)S(1)}, u32[]{:S(2)}, u32[]{:S(2)}) collective-permute-start(f32[2,28,1280]{2,1,0:T(8,128)S(1)} %get-tuple-element.59), channel_id=1, source_target_pairs={{0,8},{1,9},{2,4},{3,5},{4,2},{5,3},{6,14},{7,15},{8,0},{9,1},{10,... | collective-permute-start | bytes 860168 | tf_op jit(solution)/shard_map/ppermute | solution.py:504
  32.7 22.7 %collective-permute-start.13 = (s32[2,32,640]{2,1,0:T(8,128)S(1)}, s32[2,32,640]{2,1,0:T(8,128)S(1)}, u32[]{:S(2)}, u32[]{:S(2)}) collective-permute-start(s32[2,32,640]{2,1,0:T(8,128)S(1)} %get-tuple-element.111), channel_id=1, source_target_pairs={{0,16},{1,17},{2,18},{3,19},{4,20},{5,21},{6,22},{7,23},{8,24},{9,... | collective-permute-start | bytes 491528 | tf_op jit(solution)/shard_map/ppermute | solution.py:504
  34.2 21.1 %collective-permute-start.14 = (s32[2,32,640]{2,1,0:T(8,128)S(1)}, s32[2,32,640]{2,1,0:T(8,128)S(1)}, u32[]{:S(2)}, u32[]{:S(2)}) collective-permute-start(s32[2,32,640]{2,1,0:T(8,128)S(1)} %get-tuple-element.110), channel_id=1, source_target_pairs={{0,1},{1,0},{2,3},{3,2},{4,5},{5,4},{6,7},{7,6},{8,9},{9,8},{10,11... | collective-permute-start | bytes 491528 | tf_op jit(solution)/shard_map/ppermute | solution.py:504
  35.8 19.6 %collective-permute-start.15 = (s32[2,32,640]{2,1,0:T(8,128)S(1)}, s32[2,32,640]{2,1,0:T(8,128)S(1)}, u32[]{:S(2)}, u32[]{:S(2)}) collective-permute-start(s32[2,32,640]{2,1,0:T(8,128)S(1)} %get-tuple-element.109), channel_id=1, source_target_pairs={{0,17},{1,16},{2,19},{3,18},{4,21},{5,20},{6,23},{7,22},{8,25},{9,... | collective-permute-start | bytes 491528 | tf_op jit(solution)/shard_map/ppermute | solution.py:504
  53.5 10.7 %collective-permute-start.16 = (f32[2,28,1024]{2,1,0:T(8,128)S(1)}, f32[2,28,1024]{2,1,0:T(8,128)S(1)}, u32[]{:S(2)}, u32[]{:S(2)}) collective-permute-start(f32[2,28,1024]{2,1,0:T(8,128)S(1)} %get-tuple-element.65), channel_id=1, source_target_pairs={{0,2},{1,3},{2,0},{3,1},{4,6},{5,7},{6,4},{7,5},{8,10},{9,11},{10,... | collective-permute-start | bytes 688136 | tf_op jit(solution)/shard_map/ppermute | solution.py:504
  55.4 8.8 %collective-permute-start.17 = (f32[2,28,1024]{2,1,0:T(8,128)S(1)}, f32[2,28,1024]{2,1,0:T(8,128)S(1)}, u32[]{:S(2)}, u32[]{:S(2)}) collective-permute-start(f32[2,28,1024]{2,1,0:T(8,128)S(1)} %get-tuple-element.66), channel_id=1, source_target_pairs={{0,8},{1,9},{2,4},{3,5},{4,2},{5,3},{6,14},{7,15},{8,0},{9,1},{10,... | collective-permute-start | bytes 688136 | tf_op jit(solution)/shard_map/ppermute | solution.py:504
  56.6 11.2 %collective-permute-start.22 = (s32[1,2,64,640]{3,2,1,0:T(8,128)S(1)}, s32[1,2,64,640]{3,2,1,0:T(8,128)S(1)}, u32[]{:S(2)}, u32[]{:S(2)}) collective-permute-start(s32[1,2,64,640]{3,2,1,0:T(8,128)S(1)} %get-tuple-element.73.refs_1_), channel_id=1, source_target_pairs={{0,8},{1,9},{2,10},{3,11},{4,12},{5,13},{6,14},{7,15},{8,0},{9,1},... | collective-permute-start | bytes 983048 | tf_op jit(solution)/shard_map/ppermute | solution.py:504
  57.1 7.1 %collective-permute-start.18 = (s32[1,2,24,640]{3,2,1,0:T(8,128)S(1)}, s32[1,2,24,640]{3,2,1,0:T(8,128)S(1)}, u32[]{:S(2)}, u32[]{:S(2)}) collective-permute-start(s32[1,2,24,640]{3,2,1,0:T(8,128)S(1)} %get-tuple-element.67), channel_id=1, source_target_pairs={{0,2},{1,3},{2,0},{3,1},{4,6},{5,7},{6,4},{7,5},{8,10},{9,11},{10,... | collective-permute-start | bytes 368648 | tf_op jit(solution)/shard_map/ppermute | solution.py:504
  58.3 5.9 %collective-permute-start.19 = (s32[1,2,24,640]{3,2,1,0:T(8,128)S(1)}, s32[1,2,24,640]{3,2,1,0:T(8,128)S(1)}, u32[]{:S(2)}, u32[]{:S(2)}) collective-permute-start(s32[1,2,24,640]{3,2,1,0:T(8,128)S(1)} %get-tuple-element.68), channel_id=1, source_target_pairs={{0,8},{1,9},{2,4},{3,5},{4,2},{5,3},{6,14},{7,15},{8,0},{9,1},{10,... | collective-permute-start | bytes 368648 | tf_op jit(solution)/shard_map/ppermute | solution.py:504
  65.6 5.8 %collective-permute-start.20 = (f32[2,120,128]{2,1,0:T(8,128)S(1)}, f32[2,120,128]{2,1,0:T(8,128)S(1)}, u32[]{:S(2)}, u32[]{:S(2)}) collective-permute-start(f32[2,120,128]{2,1,0:T(8,128)S(1)} %get-tuple-element.71), channel_id=1, source_target_pairs={{0,1},{1,0},{2,3},{3,2},{4,5},{5,4},{6,7},{7,6},{8,9},{9,8},{10,11... | collective-permute-start | bytes 368648 | tf_op jit(solution)/shard_map/ppermute | solution.py:504
  67.8 18.8 %collective-permute-start.28 = (s32[2,2,24,640]{3,2,1,0:T(8,128)S(1)}, s32[2,2,24,640]{3,2,1,0:T(8,128)S(1)}, u32[]{:S(2)}, u32[]{:S(2)}) collective-permute-start(s32[2,2,24,640]{3,2,1,0:T(8,128)S(1)} %get-tuple-element.80), channel_id=1, source_target_pairs={{0,2},{1,3},{2,0},{3,1},{4,6},{5,7},{6,4},{7,5},{8,10},{9,11},{10,... | collective-permute-start | bytes 737288 | tf_op jit(solution)/shard_map/ppermute | solution.py:504
  69.6 17.0 %collective-permute-start.29 = (s32[2,2,24,640]{3,2,1,0:T(8,128)S(1)}, s32[2,2,24,640]{3,2,1,0:T(8,128)S(1)}, u32[]{:S(2)}, u32[]{:S(2)}) collective-permute-start(s32[2,2,24,640]{3,2,1,0:T(8,128)S(1)} %get-tuple-element.81), channel_id=1, source_target_pairs={{0,8},{1,9},{2,4},{3,5},{4,2},{5,3},{6,14},{7,15},{8,0},{9,1},{10,... | collective-permute-start | bytes 737288 | tf_op jit(solution)/shard_map/ppermute | solution.py:504
  69.8 26.9 %collective-permute-start.32 = (s32[2,2,64,640]{3,2,1,0:T(8,128)S(1)}, s32[2,2,64,640]{3,2,1,0:T(8,128)S(1)}, u32[]{:S(2)}, u32[]{:S(2)}) collective-permute-start(s32[2,2,64,640]{3,2,1,0:T(8,128)S(1)} %get-tuple-element.85.refs_1_), channel_id=1, source_target_pairs={{0,8},{1,9},{2,10},{3,11},{4,12},{5,13},{6,14},{7,15},{8,0},{9,1},... | collective-permute-start | bytes 1966088 | tf_op jit(solution)/shard_map/ppermute | solution.py:504
  85.0 8.5 %collective-permute-start.26 = (f32[2,28,1024]{2,1,0:T(8,128)S(1)}, f32[2,28,1024]{2,1,0:T(8,128)S(1)}, u32[]{:S(2)}, u32[]{:S(2)}) collective-permute-start(f32[2,28,1024]{2,1,0:T(8,128)S(1)} %get-tuple-element.78), channel_id=1, source_target_pairs={{0,2},{1,3},{2,0},{3,1},{4,6},{5,7},{6,4},{7,5},{8,10},{9,11},{10,... | collective-permute-start | bytes 688136 | tf_op jit(solution)/shard_map/ppermute | solution.py:504
  86.4 7.1 %collective-permute-start.27 = (f32[2,28,1024]{2,1,0:T(8,128)S(1)}, f32[2,28,1024]{2,1,0:T(8,128)S(1)}, u32[]{:S(2)}, u32[]{:S(2)}) collective-permute-start(f32[2,28,1024]{2,1,0:T(8,128)S(1)} %get-tuple-element.79), channel_id=1, source_target_pairs={{0,8},{1,9},{2,4},{3,5},{4,2},{5,3},{6,14},{7,15},{8,0},{9,1},{10,... | collective-permute-start | bytes 688136 | tf_op jit(solution)/shard_map/ppermute | solution.py:504
  94.9 5.4 %collective-permute-start.30 = (f32[2,120,128]{2,1,0:T(8,128)S(1)}, f32[2,120,128]{2,1,0:T(8,128)S(1)}, u32[]{:S(2)}, u32[]{:S(2)}) collective-permute-start(f32[2,120,128]{2,1,0:T(8,128)S(1)} %get-tuple-element.83), channel_id=1, source_target_pairs={{0,1},{1,0},{2,3},{3,2},{4,5},{5,4},{6,7},{7,6},{8,9},{9,8},{10,11... | collective-permute-start | bytes 368648 | tf_op jit(solution)/shard_map/ppermute | solution.py:504
  113.8 7.8 %collective-permute-start.36 = (f32[2,28,1024]{2,1,0:T(8,128)S(1)}, f32[2,28,1024]{2,1,0:T(8,128)S(1)}, u32[]{:S(2)}, u32[]{:S(2)}) collective-permute-start(f32[2,28,1024]{2,1,0:T(8,128)S(1)} %get-tuple-element.90), channel_id=1, source_target_pairs={{0,2},{1,3},{2,0},{3,1},{4,6},{5,7},{6,4},{7,5},{8,10},{9,11},{10,... | collective-permute-start | bytes 688136 | tf_op jit(solution)/shard_map/ppermute | solution.py:504
  115.7 5.9 %collective-permute-start.37 = (f32[2,28,1024]{2,1,0:T(8,128)S(1)}, f32[2,28,1024]{2,1,0:T(8,128)S(1)}, u32[]{:S(2)}, u32[]{:S(2)}) collective-permute-start(f32[2,28,1024]{2,1,0:T(8,128)S(1)} %get-tuple-element.91), channel_id=1, source_target_pairs={{0,8},{1,9},{2,4},{3,5},{4,2},{5,3},{6,14},{7,15},{8,0},{9,1},{10,... | collective-permute-start | bytes 688136 | tf_op jit(solution)/shard_map/ppermute | solution.py:504
  124.1 16.3 %collective-permute-start.12 = (f32[4,64,256]{2,1,0:T(8,128)S(1)}, f32[4,64,256]{2,1,0:T(8,128)S(1)}, u32[]{:S(2)}, u32[]{:S(2)}) collective-permute-start(f32[4,64,256]{2,1,0:T(8,128)S(1)} %get-tuple-element.63.refs_5_), channel_id=1, source_target_pairs={{0,8},{1,9},{2,10},{3,11},{4,12},{5,13},{6,14},{7,15},{8,0},{9,1},... | collective-permute-start | bytes 786440 | tf_op jit(solution)/shard_map/ppermute | solution.py:504
  124.6 15.8 %collective-permute-start.25 = (f32[4,64,256]{2,1,0:T(8,128)S(1)}, f32[4,64,256]{2,1,0:T(8,128)S(1)}, u32[]{:S(2)}, u32[]{:S(2)}) collective-permute-start(f32[4,64,256]{2,1,0:T(8,128)S(1)} %get-tuple-element.76), channel_id=1, source_target_pairs={{0,8},{1,9},{2,10},{3,11},{4,12},{5,13},{6,14},{7,15},{8,0},{9,1},... | collective-permute-start | bytes 786440 | tf_op jit(solution)/shard_map/ppermute | solution.py:504
  124.6 15.8 %collective-permute-start.35 = (f32[4,64,256]{2,1,0:T(8,128)S(1)}, f32[4,64,256]{2,1,0:T(8,128)S(1)}, u32[]{:S(2)}, u32[]{:S(2)}) collective-permute-start(f32[4,64,256]{2,1,0:T(8,128)S(1)} %get-tuple-element.88), channel_id=1, source_target_pairs={{0,8},{1,9},{2,10},{3,11},{4,12},{5,13},{6,14},{7,15},{8,0},{9,1},... | collective-permute-start | bytes 786440 | tf_op jit(solution)/shard_map/ppermute | solution.py:504
  142.1 6.0 %collective-permute-start.41 = (f32[4,32,256]{2,1,0:T(8,128)S(1)}, f32[4,32,256]{2,1,0:T(8,128)S(1)}, u32[]{:S(2)}, u32[]{:S(2)}) collective-permute-start(f32[4,32,256]{2,1,0:T(8,128)S(1)} %get-tuple-element.118), channel_id=1, source_target_pairs={{0,16},{1,17},{2,18},{3,19},{4,20},{5,21},{6,22},{7,23},{8,24},{9,... | collective-permute-start | bytes 393224 | tf_op jit(solution)/shard_map/ppermute | solution.py:504
  143.4 8.8 %collective-permute-start.43 = (f32[4,32,256]{2,1,0:T(8,128)S(1)}, f32[4,32,256]{2,1,0:T(8,128)S(1)}, u32[]{:S(2)}, u32[]{:S(2)}) collective-permute-start(f32[4,32,256]{2,1,0:T(8,128)S(1)} %get-tuple-element.117), channel_id=1, source_target_pairs={{0,17},{1,16},{2,19},{3,18},{4,21},{5,20},{6,23},{7,22},{8,25},{9,... | collective-permute-start | bytes 393224 | tf_op jit(solution)/shard_map/ppermute | solution.py:504
  145.7 7.9 %collective-permute-start.42 = (f32[4,32,256]{2,1,0:T(8,128)S(1)}, f32[4,32,256]{2,1,0:T(8,128)S(1)}, u32[]{:S(2)}, u32[]{:S(2)}) collective-permute-start(f32[4,32,256]{2,1,0:T(8,128)S(1)} %constant_dynamic-slice_fusion.1), channel_id=1, source_target_pairs={{0,1},{1,0},{2,3},{3,2},{4,5},{5,4},{6,7},{7,6},{8,9},{9,8},{10,11... | collective-permute-start | bytes 393224 | tf_op jit(solution)/shard_map/ppermute | solution.py:504
  (18 other events, 63.5 us)
where the time goes:
time: 155 us; the launch traced here: 154 us
  Pallas kernels  68.5 us (44%)
  waiting for transfers between devices  43.6 us (28%)
  starting transfers between devices  35.4 us (23%)
  local copies, waits for them, and re-layouts  4.77 us (3%)
  other arithmetic  1.77 us (1%)
    pallas_call x18, Pallas kernels, call(): pl.pallas_call(run, in_specs=[pl.BlockSpec(memory_space=pltpu.SMEM)] + ne...  68.5 us
    ppermute x44, waiting for transfers between devices, move(): return lax.ppermute(x, AXES, pairs)  43.6 us
    ppermute x44, starting transfers between devices, move(): return lax.ppermute(x, AXES, pairs)  35.4 us
    unnamed x12, local copies, waits for them, and re-layouts  4.54 us
  transfers between devices with their start and end apart: 44, of which 13 were waited for; matrix products, arithmetic and copies ran while one was open for 1% of the time, Pallas kernels for 35%

commit v1 on v0

--- a/solution.py
+++ b/solution.py
@@ -208,6 +208,10 @@
     whole[:, 0:strip, :] = jnp.where(first, mine[...], got[...])
     whole[:, strip : 2 * strip, :] = jnp.where(first, got[...], mine[...])
     edges_out(info, whole, send_a, send_b, halo)
+
+
+def mark_kernel(info, token):
+    token[...] = jnp.zeros_like(token)
 
 
 def columns_kernel(halo, info, mid, got_a, got_b, *refs):
@@ -529,24 +533,23 @@
     lane_t = 2 * cols + LANES
     lane_f = 4 * cols + 2 * LANES
     packed = shape(4, half, strip, lane_t, dtype=jnp.int32)
+    mine, send = call(
+        functools.partial(pack_fields_kernel, halo),
+        [shape(per_core, strip, lane_f)] * 2,
+        info,
+        source_field,
+        receiver_field,
+    )
+    got = move(send, across_side)
     keep, give = call(
         functools.partial(pack_tables_kernel, edge),
         [packed, packed],
         info,
         zone_index,
         blend_weight,
+        after=[send],
     )
     swapped = move(give, across_core)
-
-    mine, send = call(
-        functools.partial(pack_fields_kernel, halo),
-        [shape(per_core, strip, lane_f)] * 2,
-        info,
-        source_field,
-        receiver_field,
-        after=[give],
-    )
-    got = move(send, across_side)
 
     def spread(own):
         return (
@@ -605,18 +608,18 @@
         after=[give],
     )
 
-    *joined, token = join((0,), parts[0], [matrices[0]])
-    tables = finish(*joined)
-    parts[1] = spread(jnp.where(core == 1, keep, swapped))
-    whole, send_a, send_b, token = call(
+    whole, send_a, send_b, _ = call(
         functools.partial(join_fields_kernel, halo),
         [shape(per_core, rows, lane_f)] + [shape(per_core, halo, lane_f)] * 2 + [mark],
         info,
         mine,
         got,
-        after=[joined[0]],
+        after=[matrices[0]],
     )
     state = (whole, move(send_a, pairs_even), move(send_b, pairs_odd))
+    *joined, token = join((0,), parts[0], [whole])
+    tables = finish(*joined)
+    parts[1] = spread(jnp.where(core == 1, keep, swapped))
 
     area = levels * (rows + halo) * windows * LANES
     images = []
@@ -650,18 +653,21 @@
             *joined, _ = join((0,), parts[1], [image])
         field, send_a, send_b = fields
         got = [move(send_a, pairs_even), move(send_b, pairs_odd)]
+        if s == 1:
+            *handed, _ = call(mark_kernel, [mark], info, after=[image], hand=list(joined[2:]))
+            tables += finish(*joined[:2], *handed)
         *handed, side_a, side_b, token = call(
             functools.partial(columns_kernel, halo),
             [shape(per_core, rows + 2 * halo, LANES)] * 2 + [mark],
             info,
             field,
             *got,
-            hand=list(joined[2:]) if s < 2 else [],
+            after=tables[2:] if s == 1 else [],
+            hand=list(joined[2:]) if s == 0 else [],
         )
         state = (field, *got, move(side_a, across_side), move(side_b, middle))
-        if s < 2:
+        if s == 0:
             tables += finish(*joined[:2], *handed)
-        if s == 0:
             *joined, token = join((1, 1), parts[0] + parts[1], [token])
 
     sums = [x + move(x, across_core) for x in images]

time: 155 us -> 151 us (0.974)
  waiting for transfers between devices: 43.6 us -> 39.4 us
    ppermute x44, waiting for transfers between devices: 43.6 us -> 39.4 us  [move(): return lax.ppermute(x, AXES, pairs)]
    pallas_call x18 -> x19, Pallas kernels: 68.5 us -> 69.7 us  [call(): pl.pallas_call(run, in_specs=[pl.BlockSpec(memory_space=pltpu.SMEM)] + ne...]
  transfers between devices with their start and end apart: 44 -> 44, of which waited for: 13 -> 14; matrix products, arithmetic and copies ran while one was open for 1% -> 1% of each run, Pallas kernels for 35% -> 35%
where the time goes in v1:
time: 151 us
  Pallas kernels  69.7 us (46%)
  waiting for transfers between devices  39.4 us (26%)
  starting transfers between devices  34.8 us (23%)
  local copies, waits for them, and re-layouts  4.77 us (3%)
  other arithmetic  1.77 us (1%)
    pallas_call x19, Pallas kernels, call(): pl.pallas_call(run, in_specs=[pl.BlockSpec(memory_space=pltpu.SMEM)] + ne...  69.7 us
    ppermute x44, waiting for transfers between devices, move(): return lax.ppermute(x, AXES, pairs)  39.4 us
    ppermute x44, starting transfers between devices, move(): return lax.ppermute(x, AXES, pairs)  34.8 us
    unnamed x12, local copies, waits for them, and re-layouts  4.54 us
  transfers between devices with their start and end apart: 44, of which 14 were waited for; matrix products, arithmetic and copies ran while one was open for 1% of the time, Pallas kernels for 35%

profile of v1, /device:TPU:0, one launch (start us, length us, event | category | flops | bytes accessed | tf_op | source)
XLA Modules:
  0.0 150.9 jit_solution(17100573075865464017)
XLA Ops:
  3.4 3.0 %collective-permute-start.4 = (f32[2,32,1280]{2,1,0:T(8,128)S(1)}, f32[2,32,1280]{2,1,0:T(8,128)S(1)}, u32[]{:S(2)}, u32[]{:S(2)}) collective-permute-start(f32[2,32,1280]{2,1,0:T(8,128)S(1)} %get-tuple-element.50.refs_3_), channel_id=1, source_target_pairs={{0,1},{1,0},{2,3},{3,2},{4,5},{5,4},{6,7},{7,6},{8,9},{9,8},{10,11... | collective-permute-start | bytes 983048 | tf_op jit(solution)/shard_map/ppermute | solution.py:508
  9.9 1.5 %collective-permute-done = s32[4,2,32,640]{3,2,1,0:T(8,128)S(1)} collective-permute-done((s32[4,2,32,640]{3,2,1,0:T(8,128)S(1)}, s32[4,2,32,640]{3,2,1,0:T(8,128)S(1)}, u32[]{:S(2)}, u32[]{:S(2)}) %collective-permute-start) | collective-permute-done | bytes 655392 | tf_op jit(solution)/shard_map/ppermute | solution.py:508
  11.7 1.6 %collective-permute-start.1 = (s32[2,32,640]{2,1,0:T(8,128)S(1)}, s32[2,32,640]{2,1,0:T(8,128)S(1)}, u32[]{:S(2)}, u32[]{:S(2)}) collective-permute-start(s32[2,32,640]{2,1,0:T(8,128)S(1)} %get-tuple-element.115), channel_id=1, source_target_pairs={{0,16},{1,17},{2,18},{3,19},{4,20},{5,21},{6,22},{7,23},{8,24},{9,... | collective-permute-start | bytes 491528 | tf_op jit(solution)/shard_map/ppermute | solution.py:508
  13.7 1.5 collective-permute-start.3
  15.3 2.2 %shard_map.66 = (bf16[2,128,192]{2,1,0:T(8,128)(2,1)S(1)}, bf16[2,4,768,256]{3,2,1,0:T(8,128)(2,1)S(1)}) custom-call(s32[11]{0:T(128)S(1)} %stack.74.refs_0_, f32[2,4,4,128]{3,2,1,0:T(4,128)S(1)} %select_maximum_fusion.refs_1_, s32[4,2,32,640]{3,2,1,0:T(8,128)S(1)} %get-tuple-element.52.refs_2_), custom_call_target="tpu_custom_call" | custom-call | tf_op jit(solution)/shard_map/pallas_call | solution.py:455
  18.8 3.9 %collective-permute-done.2.refs_3_ = s32[2,32,640]{2,1,0:T(8,128)S(1)} collective-permute-done((s32[2,32,640]{2,1,0:T(8,128)S(1)}, s32[2,32,640]{2,1,0:T(8,128)S(1)}, u32[]{:S(2)}, u32[]{:S(2)}) %collective-permute-start.2) | collective-permute-done | bytes 163872 | tf_op jit(solution)/shard_map/ppermute | solution.py:508
  23.4 3.1 %collective-permute-start.8 = (s32[1,2,24,640]{3,2,1,0:T(8,128)S(1)}, s32[1,2,24,640]{3,2,1,0:T(8,128)S(1)}, u32[]{:S(2)}, u32[]{:S(2)}) collective-permute-start(s32[1,2,24,640]{3,2,1,0:T(8,128)S(1)} %get-tuple-element.60), channel_id=1, source_target_pairs={{0,2},{1,3},{2,0},{3,1},{4,6},{5,7},{6,4},{7,5},{8,10},{9,11},{10,... | collective-permute-start | bytes 368648 | tf_op jit(solution)/shard_map/ppermute | solution.py:508
  27.1 3.1 %collective-permute-done.8.refs_3_ = s32[1,2,24,640]{3,2,1,0:T(8,128)S(1)} collective-permute-done((s32[1,2,24,640]{3,2,1,0:T(8,128)S(1)}, s32[1,2,24,640]{3,2,1,0:T(8,128)S(1)}, u32[]{:S(2)}, u32[]{:S(2)}) %collective-permute-start.8) | collective-permute-done | bytes 122912 | tf_op jit(solution)/shard_map/ppermute | solution.py:508
  32.1 1.8 %collective-permute-start.15 = (s32[2,32,640]{2,1,0:T(8,128)S(1)}, s32[2,32,640]{2,1,0:T(8,128)S(1)}, u32[]{:S(2)}, u32[]{:S(2)}) collective-permute-start(s32[2,32,640]{2,1,0:T(8,128)S(1)} %get-tuple-element.109), channel_id=1, source_target_pairs={{0,17},{1,16},{2,19},{3,18},{4,21},{5,20},{6,23},{7,22},{8,25},{9,... | collective-permute-start | bytes 491528 | tf_op jit(solution)/shard_map/ppermute | solution.py:508
  35.2 1.5 collective-permute-done.5.refs_3_
  36.7 13.3 %shard_map.70 = (f32[4,64,256]{2,1,0:T(8,128)S(1)}, f32[2,64,1024]{2,1,0:T(8,128)S(1)}, f32[2,28,1024]{2,1,0:T(8,128)S(1)}, f32[2,28,1024]{2,1,0:T(8,128)S(1)}) custom-call(s32[11]{0:T(128)S(1)} %stack.74.refs_0_, f32[8,128]{1,0:T(8,128)S(1)} %get-tuple-element.56.refs_1_, f32[2,64,1280]{2,1,0:T(8,128)S(1)} %get-tuple-element.55.refs_5_.refs_2_, ...), custom_call_target="tpu_custom_call" | custom-call | flops 13891534848 | bytes 2097152 | tf_op jit(solution)/shard_map/pallas_call | solution.py:455
  50.0 1.8 %collective-permute-start.16 = (f32[2,28,1024]{2,1,0:T(8,128)S(1)}, f32[2,28,1024]{2,1,0:T(8,128)S(1)}, u32[]{:S(2)}, u32[]{:S(2)}) collective-permute-start(f32[2,28,1024]{2,1,0:T(8,128)S(1)} %get-tuple-element.65), channel_id=1, source_target_pairs={{0,2},{1,3},{2,0},{3,1},{4,6},{5,7},{6,4},{7,5},{8,10},{9,11},{10,... | collective-permute-start | bytes 688136 | tf_op jit(solution)/shard_map/ppermute | solution.py:508
  53.5 2.0 %collective-permute-start.18 = (s32[1,2,24,640]{3,2,1,0:T(8,128)S(1)}, s32[1,2,24,640]{3,2,1,0:T(8,128)S(1)}, u32[]{:S(2)}, u32[]{:S(2)}) collective-permute-start(s32[1,2,24,640]{3,2,1,0:T(8,128)S(1)} %get-tuple-element.67), channel_id=1, source_target_pairs={{0,2},{1,3},{2,0},{3,1},{4,6},{5,7},{6,4},{7,5},{8,10},{9,11},{10,... | collective-permute-start | bytes 368648 | tf_op jit(solution)/shard_map/ppermute | solution.py:508
  55.7 4.9 %collective-permute-done.18.refs_4_ = s32[1,2,24,640]{3,2,1,0:T(8,128)S(1)} collective-permute-done((s32[1,2,24,640]{3,2,1,0:T(8,128)S(1)}, s32[1,2,24,640]{3,2,1,0:T(8,128)S(1)}, u32[]{:S(2)}, u32[]{:S(2)}) %collective-permute-start.18) | collective-permute-done | bytes 122912 | tf_op jit(solution)/shard_map/ppermute | solution.py:508
  63.4 2.2 %collective-permute-start.29 = (s32[2,2,24,640]{3,2,1,0:T(8,128)S(1)}, s32[2,2,24,640]{3,2,1,0:T(8,128)S(1)}, u32[]{:S(2)}, u32[]{:S(2)}) collective-permute-start(s32[2,2,24,640]{3,2,1,0:T(8,128)S(1)} %get-tuple-element.81), channel_id=1, source_target_pairs={{0,2},{1,3},{2,0},{3,1},{4,6},{5,7},{6,4},{7,5},{8,10},{9,11},{10,... | collective-permute-start | bytes 737288 | tf_op jit(solution)/shard_map/ppermute | solution.py:508
  67.5 13.3 %shard_map.75 = (f32[4,64,256]{2,1,0:T(8,128)S(1)}, f32[2,64,1024]{2,1,0:T(8,128)S(1)}, f32[2,28,1024]{2,1,0:T(8,128)S(1)}, f32[2,28,1024]{2,1,0:T(8,128)S(1)}) custom-call(s32[11]{0:T(128)S(1)} %stack.74.refs_0_, f32[8,128]{1,0:T(8,128)S(1)} %get-tuple-element.70.refs_1_, f32[2,64,1024]{2,1,0:T(8,128)S(1)} %get-tuple-element.64.refs_1_.refs_2_, ...), custom_call_target="tpu_custom_call" | custom-call | flops 13891534848 | bytes 2097152 | tf_op jit(solution)/shard_map/pallas_call | solution.py:455
  82.5 2.0 %collective-permute-start.26 = (f32[2,28,1024]{2,1,0:T(8,128)S(1)}, f32[2,28,1024]{2,1,0:T(8,128)S(1)}, u32[]{:S(2)}, u32[]{:S(2)}) collective-permute-start(f32[2,28,1024]{2,1,0:T(8,128)S(1)} %get-tuple-element.78), channel_id=1, source_target_pairs={{0,2},{1,3},{2,0},{3,1},{4,6},{5,7},{6,4},{7,5},{8,10},{9,11},{10,... | collective-permute-start | bytes 688136 | tf_op jit(solution)/shard_map/ppermute | solution.py:508
  87.2 3.8 %collective-permute-done.26.refs_2_.refs_3_ = f32[2,28,1024]{2,1,0:T(8,128)S(1)} collective-permute-done((f32[2,28,1024]{2,1,0:T(8,128)S(1)}, f32[2,28,1024]{2,1,0:T(8,128)S(1)}, u32[]{:S(2)}, u32[]{:S(2)}) %collective-permute-start.26) | collective-permute-done | bytes 229408 | tf_op jit(solution)/shard_map/ppermute | solution.py:508
  91.9 2.1 %collective-permute-start.33 = (f32[2,120,128]{2,1,0:T(8,128)S(1)}, f32[2,120,128]{2,1,0:T(8,128)S(1)}, u32[]{:S(2)}, u32[]{:S(2)}) collective-permute-start(f32[2,120,128]{2,1,0:T(8,128)S(1)} %get-tuple-element.86), channel_id=1, source_target_pairs={{0,1},{1,0},{2,3},{3,2},{4,5},{5,4},{6,7},{7,6},{8,9},{9,8},{10,11... | collective-permute-start | bytes 368648 | tf_op jit(solution)/shard_map/ppermute | solution.py:508
  94.0 3.0 %collective-permute-done.33.refs_5_ = f32[2,120,128]{2,1,0:T(8,128)S(1)} collective-permute-done((f32[2,120,128]{2,1,0:T(8,128)S(1)}, f32[2,120,128]{2,1,0:T(8,128)S(1)}, u32[]{:S(2)}, u32[]{:S(2)}) %collective-permute-start.33) | collective-permute-done | bytes 122912 | tf_op jit(solution)/shard_map/ppermute | solution.py:508
  96.9 13.5 %shard_map.80 = (f32[4,64,256]{2,1,0:T(8,128)S(1)}, f32[2,64,1024]{2,1,0:T(8,128)S(1)}, f32[2,28,1024]{2,1,0:T(8,128)S(1)}, f32[2,28,1024]{2,1,0:T(8,128)S(1)}) custom-call(s32[11]{0:T(128)S(1)} %stack.74.refs_0_, f32[8,128]{1,0:T(8,128)S(1)} %get-tuple-element.85.refs_1_, f32[2,64,1024]{2,1,0:T(8,128)S(1)} %get-tuple-element.77.refs_1_.refs_2_, ...), custom_call_target="tpu_custom_call" | custom-call | flops 13891534848 | bytes 2097152 | tf_op jit(solution)/shard_map/pallas_call | solution.py:455
  110.5 1.9 %collective-permute-start.36 = (f32[2,28,1024]{2,1,0:T(8,128)S(1)}, f32[2,28,1024]{2,1,0:T(8,128)S(1)}, u32[]{:S(2)}, u32[]{:S(2)}) collective-permute-start(f32[2,28,1024]{2,1,0:T(8,128)S(1)} %get-tuple-element.90), channel_id=1, source_target_pairs={{0,2},{1,3},{2,0},{3,1},{4,6},{5,7},{6,4},{7,5},{8,10},{9,11},{10,... | collective-permute-start | bytes 688136 | tf_op jit(solution)/shard_map/ppermute | solution.py:508
  112.3 5.4 %collective-permute-done.36.refs_2_.refs_3_ = f32[2,28,1024]{2,1,0:T(8,128)S(1)} collective-permute-done((f32[2,28,1024]{2,1,0:T(8,128)S(1)}, f32[2,28,1024]{2,1,0:T(8,128)S(1)}, u32[]{:S(2)}, u32[]{:S(2)}) %collective-permute-start.36) | collective-permute-done | bytes 229408 | tf_op jit(solution)/shard_map/ppermute | solution.py:508
  118.6 1.5 collective-permute-start.38
  121.1 2.5 %collective-permute-done.38.refs_5_ = f32[2,120,128]{2,1,0:T(8,128)S(1)} collective-permute-done((f32[2,120,128]{2,1,0:T(8,128)S(1)}, f32[2,120,128]{2,1,0:T(8,128)S(1)}, u32[]{:S(2)}, u32[]{:S(2)}) %collective-permute-start.38) | collective-permute-done | bytes 122912 | tf_op jit(solution)/shard_map/ppermute | solution.py:508
  123.5 12.9 %shard_map.82 = f32[4,64,256]{2,1,0:T(8,128)S(1)} custom-call(s32[11]{0:T(128)S(1)} %stack.74.refs_0_, f32[8,128]{1,0:T(8,128)S(1)} %get-tuple-element.92.refs_1_, f32[2,64,1024]{2,1,0:T(8,128)S(1)} %get-tuple-element.89.refs_1_.refs_2_, f32[2,28,1024]{2,1,0:T(8,128)S(1)} %collective-permute-done.36.refs_2_.refs_3_, ...), custom_call_target="tpu_custom_call" | custom-call | flops 13891534848 | bytes 2097152 | tf_op jit(solution)/shard_map/pallas_call | solution.py:455
  136.5 1.5 collective-permute-done.40
  138.2 2.0 %collective-permute-start.41 = (f32[4,32,256]{2,1,0:T(8,128)S(1)}, f32[4,32,256]{2,1,0:T(8,128)S(1)}, u32[]{:S(2)}, u32[]{:S(2)}) collective-permute-start(f32[4,32,256]{2,1,0:T(8,128)S(1)} %get-tuple-element.118), channel_id=1, source_target_pairs={{0,16},{1,17},{2,18},{3,19},{4,20},{5,21},{6,22},{7,23},{8,24},{9,... | collective-permute-start | bytes 393224 | tf_op jit(solution)/shard_map/ppermute | solution.py:508
  140.2 1.6 %collective-permute-start.43 = (f32[4,32,256]{2,1,0:T(8,128)S(1)}, f32[4,32,256]{2,1,0:T(8,128)S(1)}, u32[]{:S(2)}, u32[]{:S(2)}) collective-permute-start(f32[4,32,256]{2,1,0:T(8,128)S(1)} %get-tuple-element.117), channel_id=1, source_target_pairs={{0,17},{1,16},{2,19},{3,18},{4,21},{5,20},{6,23},{7,22},{8,25},{9,... | collective-permute-start | bytes 393224 | tf_op jit(solution)/shard_map/ppermute | solution.py:508
  142.3 1.8 %collective-permute-done.41 = f32[4,32,256]{2,1,0:T(8,128)S(1)} collective-permute-done((f32[4,32,256]{2,1,0:T(8,128)S(1)}, f32[4,32,256]{2,1,0:T(8,128)S(1)}, u32[]{:S(2)}, u32[]{:S(2)}) %collective-permute-start.41) | collective-permute-done | bytes 131104 | tf_op jit(solution)/shard_map/ppermute | solution.py:508
  144.1 4.3 %collective-permute-done.43 = f32[4,32,256]{2,1,0:T(8,128)S(1)} collective-permute-done((f32[4,32,256]{2,1,0:T(8,128)S(1)}, f32[4,32,256]{2,1,0:T(8,128)S(1)}, u32[]{:S(2)}, u32[]{:S(2)}) %collective-permute-start.43) | collective-permute-done | bytes 131104 | tf_op jit(solution)/shard_map/ppermute | solution.py:508
  148.4 1.5 collective-permute-done.42
  (107 shorter events, 28.5 us)
Async XLA Ops:
  3.4 14.2 %collective-permute-start.4 = (f32[2,32,1280]{2,1,0:T(8,128)S(1)}, f32[2,32,1280]{2,1,0:T(8,128)S(1)}, u32[]{:S(2)}, u32[]{:S(2)}) collective-permute-start(f32[2,32,1280]{2,1,0:T(8,128)S(1)} %get-tuple-element.50.refs_3_), channel_id=1, source_target_pairs={{0,1},{1,0},{2,3},{3,2},{4,5},{5,4},{6,7},{7,6},{8,9},{9,8},{10,11... | collective-permute-start | bytes 983048 | tf_op jit(solution)/shard_map/ppermute | solution.py:508
  11.7 7.2 %collective-permute-start.1 = (s32[2,32,640]{2,1,0:T(8,128)S(1)}, s32[2,32,640]{2,1,0:T(8,128)S(1)}, u32[]{:S(2)}, u32[]{:S(2)}) collective-permute-start(s32[2,32,640]{2,1,0:T(8,128)S(1)} %get-tuple-element.115), channel_id=1, source_target_pairs={{0,16},{1,17},{2,18},{3,19},{4,20},{5,21},{6,22},{7,23},{8,24},{9,... | collective-permute-start | bytes 491528 | tf_op jit(solution)/shard_map/ppermute | solution.py:508
  13.2 9.5 %collective-permute-start.2 = (s32[2,32,640]{2,1,0:T(8,128)S(1)}, s32[2,32,640]{2,1,0:T(8,128)S(1)}, u32[]{:S(2)}, u32[]{:S(2)}) collective-permute-start(s32[2,32,640]{2,1,0:T(8,128)S(1)} %get-tuple-element.114), channel_id=1, source_target_pairs={{0,1},{1,0},{2,3},{3,2},{4,5},{5,4},{6,7},{7,6},{8,9},{9,8},{10,11... | collective-permute-start | bytes 491528 | tf_op jit(solution)/shard_map/ppermute | solution.py:508
  13.7 9.0 %collective-permute-start.3 = (s32[2,32,640]{2,1,0:T(8,128)S(1)}, s32[2,32,640]{2,1,0:T(8,128)S(1)}, u32[]{:S(2)}, u32[]{:S(2)}) collective-permute-start(s32[2,32,640]{2,1,0:T(8,128)S(1)} %get-tuple-element.113), channel_id=1, source_target_pairs={{0,17},{1,16},{2,19},{3,18},{4,21},{5,20},{6,23},{7,22},{8,25},{9,... | collective-permute-start | bytes 491528 | tf_op jit(solution)/shard_map/ppermute | solution.py:508
  23.4 6.9 %collective-permute-start.8 = (s32[1,2,24,640]{3,2,1,0:T(8,128)S(1)}, s32[1,2,24,640]{3,2,1,0:T(8,128)S(1)}, u32[]{:S(2)}, u32[]{:S(2)}) collective-permute-start(s32[1,2,24,640]{3,2,1,0:T(8,128)S(1)} %get-tuple-element.60), channel_id=1, source_target_pairs={{0,2},{1,3},{2,0},{3,1},{4,6},{5,7},{6,4},{7,5},{8,10},{9,11},{10,... | collective-permute-start | bytes 368648 | tf_op jit(solution)/shard_map/ppermute | solution.py:508
  26.5 5.6 %collective-permute-start.7 = (s32[1,2,64,640]{3,2,1,0:T(8,128)S(1)}, s32[1,2,64,640]{3,2,1,0:T(8,128)S(1)}, u32[]{:S(2)}, u32[]{:S(2)}) collective-permute-start(s32[1,2,64,640]{3,2,1,0:T(8,128)S(1)} %get-tuple-element.59.refs_1_), channel_id=1, source_target_pairs={{0,8},{1,9},{2,10},{3,11},{4,12},{5,13},{6,14},{7,15},{8,0},{9,1},... | collective-permute-start | bytes 983048 | tf_op jit(solution)/shard_map/ppermute | solution.py:508
  26.5 10.1 %collective-permute-start.5 = (f32[2,28,1280]{2,1,0:T(8,128)S(1)}, f32[2,28,1280]{2,1,0:T(8,128)S(1)}, u32[]{:S(2)}, u32[]{:S(2)}) collective-permute-start(f32[2,28,1280]{2,1,0:T(8,128)S(1)} %get-tuple-element.57), channel_id=1, source_target_pairs={{0,2},{1,3},{2,0},{3,1},{4,6},{5,7},{6,4},{7,5},{8,10},{9,11},{10,... | collective-permute-start | bytes 860168 | tf_op jit(solution)/shard_map/ppermute | solution.py:508
  26.6 10.1 %collective-permute-start.6 = (f32[2,28,1280]{2,1,0:T(8,128)S(1)}, f32[2,28,1280]{2,1,0:T(8,128)S(1)}, u32[]{:S(2)}, u32[]{:S(2)}) collective-permute-start(f32[2,28,1280]{2,1,0:T(8,128)S(1)} %get-tuple-element.58), channel_id=1, source_target_pairs={{0,8},{1,9},{2,4},{3,5},{4,2},{5,3},{6,14},{7,15},{8,0},{9,1},{10,... | collective-permute-start | bytes 860168 | tf_op jit(solution)/shard_map/ppermute | solution.py:508
  30.3 21.5 %collective-permute-start.13 = (s32[2,32,640]{2,1,0:T(8,128)S(1)}, s32[2,32,640]{2,1,0:T(8,128)S(1)}, u32[]{:S(2)}, u32[]{:S(2)}) collective-permute-start(s32[2,32,640]{2,1,0:T(8,128)S(1)} %get-tuple-element.111), channel_id=1, source_target_pairs={{0,16},{1,17},{2,18},{3,19},{4,20},{5,21},{6,22},{7,23},{8,24},{9,... | collective-permute-start | bytes 491528 | tf_op jit(solution)/shard_map/ppermute | solution.py:508
  31.6 20.2 %collective-permute-start.14 = (s32[2,32,640]{2,1,0:T(8,128)S(1)}, s32[2,32,640]{2,1,0:T(8,128)S(1)}, u32[]{:S(2)}, u32[]{:S(2)}) collective-permute-start(s32[2,32,640]{2,1,0:T(8,128)S(1)} %get-tuple-element.110), channel_id=1, source_target_pairs={{0,1},{1,0},{2,3},{3,2},{4,5},{5,4},{6,7},{7,6},{8,9},{9,8},{10,11... | collective-permute-start | bytes 491528 | tf_op jit(solution)/shard_map/ppermute | solution.py:508
  32.1 19.7 %collective-permute-start.15 = (s32[2,32,640]{2,1,0:T(8,128)S(1)}, s32[2,32,640]{2,1,0:T(8,128)S(1)}, u32[]{:S(2)}, u32[]{:S(2)}) collective-permute-start(s32[2,32,640]{2,1,0:T(8,128)S(1)} %get-tuple-element.109), channel_id=1, source_target_pairs={{0,17},{1,16},{2,19},{3,18},{4,21},{5,20},{6,23},{7,22},{8,25},{9,... | collective-permute-start | bytes 491528 | tf_op jit(solution)/shard_map/ppermute | solution.py:508
  50.0 10.6 %collective-permute-start.16 = (f32[2,28,1024]{2,1,0:T(8,128)S(1)}, f32[2,28,1024]{2,1,0:T(8,128)S(1)}, u32[]{:S(2)}, u32[]{:S(2)}) collective-permute-start(f32[2,28,1024]{2,1,0:T(8,128)S(1)} %get-tuple-element.65), channel_id=1, source_target_pairs={{0,2},{1,3},{2,0},{3,1},{4,6},{5,7},{6,4},{7,5},{8,10},{9,11},{10,... | collective-permute-start | bytes 688136 | tf_op jit(solution)/shard_map/ppermute | solution.py:508
  51.8 8.8 %collective-permute-start.17 = (f32[2,28,1024]{2,1,0:T(8,128)S(1)}, f32[2,28,1024]{2,1,0:T(8,128)S(1)}, u32[]{:S(2)}, u32[]{:S(2)}) collective-permute-start(f32[2,28,1024]{2,1,0:T(8,128)S(1)} %get-tuple-element.66), channel_id=1, source_target_pairs={{0,8},{1,9},{2,4},{3,5},{4,2},{5,3},{6,14},{7,15},{8,0},{9,1},{10,... | collective-permute-start | bytes 688136 | tf_op jit(solution)/shard_map/ppermute | solution.py:508
  53.0 10.4 %collective-permute-start.22 = (s32[1,2,64,640]{3,2,1,0:T(8,128)S(1)}, s32[1,2,64,640]{3,2,1,0:T(8,128)S(1)}, u32[]{:S(2)}, u32[]{:S(2)}) collective-permute-start(s32[1,2,64,640]{3,2,1,0:T(8,128)S(1)} %get-tuple-element.73.refs_1_), channel_id=1, source_target_pairs={{0,8},{1,9},{2,10},{3,11},{4,12},{5,13},{6,14},{7,15},{8,0},{9,1},... | collective-permute-start | bytes 983048 | tf_op jit(solution)/shard_map/ppermute | solution.py:508
  53.5 7.1 %collective-permute-start.18 = (s32[1,2,24,640]{3,2,1,0:T(8,128)S(1)}, s32[1,2,24,640]{3,2,1,0:T(8,128)S(1)}, u32[]{:S(2)}, u32[]{:S(2)}) collective-permute-start(s32[1,2,24,640]{3,2,1,0:T(8,128)S(1)} %get-tuple-element.67), channel_id=1, source_target_pairs={{0,2},{1,3},{2,0},{3,1},{4,6},{5,7},{6,4},{7,5},{8,10},{9,11},{10,... | collective-permute-start | bytes 368648 | tf_op jit(solution)/shard_map/ppermute | solution.py:508
  55.5 5.1 %collective-permute-start.19 = (s32[1,2,24,640]{3,2,1,0:T(8,128)S(1)}, s32[1,2,24,640]{3,2,1,0:T(8,128)S(1)}, u32[]{:S(2)}, u32[]{:S(2)}) collective-permute-start(s32[1,2,24,640]{3,2,1,0:T(8,128)S(1)} %get-tuple-element.68), channel_id=1, source_target_pairs={{0,8},{1,9},{2,4},{3,5},{4,2},{5,3},{6,14},{7,15},{8,0},{9,1},{10,... | collective-permute-start | bytes 368648 | tf_op jit(solution)/shard_map/ppermute | solution.py:508
  62.1 5.4 %collective-permute-start.20 = (f32[2,120,128]{2,1,0:T(8,128)S(1)}, f32[2,120,128]{2,1,0:T(8,128)S(1)}, u32[]{:S(2)}, u32[]{:S(2)}) collective-permute-start(f32[2,120,128]{2,1,0:T(8,128)S(1)} %get-tuple-element.71), channel_id=1, source_target_pairs={{0,1},{1,0},{2,3},{3,2},{4,5},{5,4},{6,7},{7,6},{8,9},{9,8},{10,11... | collective-permute-start | bytes 368648 | tf_op jit(solution)/shard_map/ppermute | solution.py:508
  63.4 17.4 %collective-permute-start.29 = (s32[2,2,24,640]{3,2,1,0:T(8,128)S(1)}, s32[2,2,24,640]{3,2,1,0:T(8,128)S(1)}, u32[]{:S(2)}, u32[]{:S(2)}) collective-permute-start(s32[2,2,24,640]{3,2,1,0:T(8,128)S(1)} %get-tuple-element.81), channel_id=1, source_target_pairs={{0,2},{1,3},{2,0},{3,1},{4,6},{5,7},{6,4},{7,5},{8,10},{9,11},{10,... | collective-permute-start | bytes 737288 | tf_op jit(solution)/shard_map/ppermute | solution.py:508
  65.6 15.2 %collective-permute-start.30 = (s32[2,2,24,640]{3,2,1,0:T(8,128)S(1)}, s32[2,2,24,640]{3,2,1,0:T(8,128)S(1)}, u32[]{:S(2)}, u32[]{:S(2)}) collective-permute-start(s32[2,2,24,640]{3,2,1,0:T(8,128)S(1)} %get-tuple-element.82), channel_id=1, source_target_pairs={{0,8},{1,9},{2,4},{3,5},{4,2},{5,3},{6,14},{7,15},{8,0},{9,1},{10,... | collective-permute-start | bytes 737288 | tf_op jit(solution)/shard_map/ppermute | solution.py:508
  65.9 18.7 %collective-permute-start.28 = (s32[2,2,64,640]{3,2,1,0:T(8,128)S(1)}, s32[2,2,64,640]{3,2,1,0:T(8,128)S(1)}, u32[]{:S(2)}, u32[]{:S(2)}) collective-permute-start(s32[2,2,64,640]{3,2,1,0:T(8,128)S(1)} %get-tuple-element.80.refs_1_), channel_id=1, source_target_pairs={{0,8},{1,9},{2,10},{3,11},{4,12},{5,13},{6,14},{7,15},{8,0},{9,1},... | collective-permute-start | bytes 1966088 | tf_op jit(solution)/shard_map/ppermute | solution.py:508
  82.5 8.5 %collective-permute-start.26 = (f32[2,28,1024]{2,1,0:T(8,128)S(1)}, f32[2,28,1024]{2,1,0:T(8,128)S(1)}, u32[]{:S(2)}, u32[]{:S(2)}) collective-permute-start(f32[2,28,1024]{2,1,0:T(8,128)S(1)} %get-tuple-element.78), channel_id=1, source_target_pairs={{0,2},{1,3},{2,0},{3,1},{4,6},{5,7},{6,4},{7,5},{8,10},{9,11},{10,... | collective-permute-start | bytes 688136 | tf_op jit(solution)/shard_map/ppermute | solution.py:508
  84.5 6.5 %collective-permute-start.27 = (f32[2,28,1024]{2,1,0:T(8,128)S(1)}, f32[2,28,1024]{2,1,0:T(8,128)S(1)}, u32[]{:S(2)}, u32[]{:S(2)}) collective-permute-start(f32[2,28,1024]{2,1,0:T(8,128)S(1)} %get-tuple-element.79), channel_id=1, source_target_pairs={{0,8},{1,9},{2,4},{3,5},{4,2},{5,3},{6,14},{7,15},{8,0},{9,1},{10,... | collective-permute-start | bytes 688136 | tf_op jit(solution)/shard_map/ppermute | solution.py:508
  91.9 5.1 %collective-permute-start.33 = (f32[2,120,128]{2,1,0:T(8,128)S(1)}, f32[2,120,128]{2,1,0:T(8,128)S(1)}, u32[]{:S(2)}, u32[]{:S(2)}) collective-permute-start(f32[2,120,128]{2,1,0:T(8,128)S(1)} %get-tuple-element.86), channel_id=1, source_target_pairs={{0,1},{1,0},{2,3},{3,2},{4,5},{5,4},{6,7},{7,6},{8,9},{9,8},{10,11... | collective-permute-start | bytes 368648 | tf_op jit(solution)/shard_map/ppermute | solution.py:508
  110.5 7.2 %collective-permute-start.36 = (f32[2,28,1024]{2,1,0:T(8,128)S(1)}, f32[2,28,1024]{2,1,0:T(8,128)S(1)}, u32[]{:S(2)}, u32[]{:S(2)}) collective-permute-start(f32[2,28,1024]{2,1,0:T(8,128)S(1)} %get-tuple-element.90), channel_id=1, source_target_pairs={{0,2},{1,3},{2,0},{3,1},{4,6},{5,7},{6,4},{7,5},{8,10},{9,11},{10,... | collective-permute-start | bytes 688136 | tf_op jit(solution)/shard_map/ppermute | solution.py:508
  112.3 5.4 %collective-permute-start.37 = (f32[2,28,1024]{2,1,0:T(8,128)S(1)}, f32[2,28,1024]{2,1,0:T(8,128)S(1)}, u32[]{:S(2)}, u32[]{:S(2)}) collective-permute-start(f32[2,28,1024]{2,1,0:T(8,128)S(1)} %get-tuple-element.91), channel_id=1, source_target_pairs={{0,8},{1,9},{2,4},{3,5},{4,2},{5,3},{6,14},{7,15},{8,0},{9,1},{10,... | collective-permute-start | bytes 688136 | tf_op jit(solution)/shard_map/ppermute | solution.py:508
  118.6 4.9 %collective-permute-start.38 = (f32[2,120,128]{2,1,0:T(8,128)S(1)}, f32[2,120,128]{2,1,0:T(8,128)S(1)}, u32[]{:S(2)}, u32[]{:S(2)}) collective-permute-start(f32[2,120,128]{2,1,0:T(8,128)S(1)} %get-tuple-element.93), channel_id=1, source_target_pairs={{0,1},{1,0},{2,3},{3,2},{4,5},{5,4},{6,7},{7,6},{8,9},{9,8},{10,11... | collective-permute-start | bytes 368648 | tf_op jit(solution)/shard_map/ppermute | solution.py:508
  120.0 16.5 %collective-permute-start.12 = (f32[4,64,256]{2,1,0:T(8,128)S(1)}, f32[4,64,256]{2,1,0:T(8,128)S(1)}, u32[]{:S(2)}, u32[]{:S(2)}) collective-permute-start(f32[4,64,256]{2,1,0:T(8,128)S(1)} %get-tuple-element.63.refs_5_), channel_id=1, source_target_pairs={{0,8},{1,9},{2,10},{3,11},{4,12},{5,13},{6,14},{7,15},{8,0},{9,1},... | collective-permute-start | bytes 786440 | tf_op jit(solution)/shard_map/ppermute | solution.py:508
  120.5 16.0 %collective-permute-start.25 = (f32[4,64,256]{2,1,0:T(8,128)S(1)}, f32[4,64,256]{2,1,0:T(8,128)S(1)}, u32[]{:S(2)}, u32[]{:S(2)}) collective-permute-start(f32[4,64,256]{2,1,0:T(8,128)S(1)} %get-tuple-element.76.refs_1_), channel_id=1, source_target_pairs={{0,8},{1,9},{2,10},{3,11},{4,12},{5,13},{6,14},{7,15},{8,0},{9,1},... | collective-permute-start | bytes 786440 | tf_op jit(solution)/shard_map/ppermute | solution.py:508
  120.5 16.0 %collective-permute-start.35 = (f32[4,64,256]{2,1,0:T(8,128)S(1)}, f32[4,64,256]{2,1,0:T(8,128)S(1)}, u32[]{:S(2)}, u32[]{:S(2)}) collective-permute-start(f32[4,64,256]{2,1,0:T(8,128)S(1)} %get-tuple-element.88), channel_id=1, source_target_pairs={{0,8},{1,9},{2,10},{3,11},{4,12},{5,13},{6,14},{7,15},{8,0},{9,1},... | collective-permute-start | bytes 786440 | tf_op jit(solution)/shard_map/ppermute | solution.py:508
  138.2 5.9 %collective-permute-start.41 = (f32[4,32,256]{2,1,0:T(8,128)S(1)}, f32[4,32,256]{2,1,0:T(8,128)S(1)}, u32[]{:S(2)}, u32[]{:S(2)}) collective-permute-start(f32[4,32,256]{2,1,0:T(8,128)S(1)} %get-tuple-element.118), channel_id=1, source_target_pairs={{0,16},{1,17},{2,18},{3,19},{4,20},{5,21},{6,22},{7,23},{8,24},{9,... | collective-permute-start | bytes 393224 | tf_op jit(solution)/shard_map/ppermute | solution.py:508
  140.2 8.2 %collective-permute-start.43 = (f32[4,32,256]{2,1,0:T(8,128)S(1)}, f32[4,32,256]{2,1,0:T(8,128)S(1)}, u32[]{:S(2)}, u32[]{:S(2)}) collective-permute-start(f32[4,32,256]{2,1,0:T(8,128)S(1)} %get-tuple-element.117), channel_id=1, source_target_pairs={{0,17},{1,16},{2,19},{3,18},{4,21},{5,20},{6,23},{7,22},{8,25},{9,... | collective-permute-start | bytes 393224 | tf_op jit(solution)/shard_map/ppermute | solution.py:508
  141.8 8.1 %collective-permute-start.42 = (f32[4,32,256]{2,1,0:T(8,128)S(1)}, f32[4,32,256]{2,1,0:T(8,128)S(1)}, u32[]{:S(2)}, u32[]{:S(2)}) collective-permute-start(f32[4,32,256]{2,1,0:T(8,128)S(1)} %constant_dynamic-slice_fusion.1), channel_id=1, source_target_pairs={{0,1},{1,0},{2,3},{3,2},{4,5},{5,4},{6,7},{7,6},{8,9},{9,8},{10,11... | collective-permute-start | bytes 393224 | tf_op jit(solution)/shard_map/ppermute | solution.py:508
  (18 other events, 60.3 us)

commit v2 on v1

--- a/solution.py
+++ b/solution.py
@@ -338,13 +338,13 @@
                 ],
                 axis=1,
             )
+            if held > height:
+                x = jnp.concatenate([x, jnp.zeros((held - height, x.shape[1]), f32)], axis=0)
             for b in range(windows):
                 high, low = split(window(x, 0, b))
                 at = (f * windows + b) * LANES
-                cur_ref[p, 0, 0:height, at : at + LANES] = high
-                cur_ref[p, 1, 0:height, at : at + LANES] = low
-    if held > height:
-        cur_ref[:, :, height:held, :] = jnp.zeros((2, 2, held - height, 2 * lanes), bf16)
+                cur_ref[p, 0, :, at : at + LANES] = high
+                cur_ref[p, 1, :, at : at + LANES] = low
     lane = lax.broadcasted_iota(jnp.int32, (BLK, LANES), 1)
 
     def chunk(l, base, blocks):

time: 151 us -> 151 us (level)
  no operation moved by 1% of the time
where the time goes in v2:
time: 151 us
  Pallas kernels  69.8 us (46%)
  waiting for transfers between devices  39.4 us (26%)
  starting transfers between devices  34.8 us (23%)
  local copies, waits for them, and re-layouts  4.77 us (3%)
  other arithmetic  1.77 us (1%)
    pallas_call x19, Pallas kernels, call(): pl.pallas_call(run, in_specs=[pl.BlockSpec(memory_space=pltpu.SMEM)] + ne...  69.8 us
    ppermute x44, waiting for transfers between devices, move(): return lax.ppermute(x, AXES, pairs)  39.4 us
    ppermute x44, starting transfers between devices, move(): return lax.ppermute(x, AXES, pairs)  34.8 us
    unnamed x12, local copies, waits for them, and re-layouts  4.54 us
  transfers between devices with their start and end apart: 44, of which 14 were waited for; matrix products, arithmetic and copies ran while one was open for 1% of the time, Pallas kernels for 35%

profile of v2, /device:TPU:0, one launch (start us, length us, event | category | flops | bytes accessed | tf_op | source)
XLA Modules:
  0.0 150.9 jit_solution(18064401303238437615)
XLA Ops:
  3.4 3.0 %collective-permute-start.4 = (f32[2,32,1280]{2,1,0:T(8,128)S(1)}, f32[2,32,1280]{2,1,0:T(8,128)S(1)}, u32[]{:S(2)}, u32[]{:S(2)}) collective-permute-start(f32[2,32,1280]{2,1,0:T(8,128)S(1)} %get-tuple-element.50.refs_3_), channel_id=1, source_target_pairs={{0,1},{1,0},{2,3},{3,2},{4,5},{5,4},{6,7},{7,6},{8,9},{9,8},{10,11... | collective-permute-start | bytes 983048 | tf_op jit(solution)/shard_map/ppermute | solution.py:508
  9.9 1.5 %collective-permute-done = s32[4,2,32,640]{3,2,1,0:T(8,128)S(1)} collective-permute-done((s32[4,2,32,640]{3,2,1,0:T(8,128)S(1)}, s32[4,2,32,640]{3,2,1,0:T(8,128)S(1)}, u32[]{:S(2)}, u32[]{:S(2)}) %collective-permute-start) | collective-permute-done | bytes 655392 | tf_op jit(solution)/shard_map/ppermute | solution.py:508
  11.7 1.6 %collective-permute-start.1 = (s32[2,32,640]{2,1,0:T(8,128)S(1)}, s32[2,32,640]{2,1,0:T(8,128)S(1)}, u32[]{:S(2)}, u32[]{:S(2)}) collective-permute-start(s32[2,32,640]{2,1,0:T(8,128)S(1)} %get-tuple-element.115), channel_id=1, source_target_pairs={{0,16},{1,17},{2,18},{3,19},{4,20},{5,21},{6,22},{7,23},{8,24},{9,... | collective-permute-start | bytes 491528 | tf_op jit(solution)/shard_map/ppermute | solution.py:508
  13.7 1.5 collective-permute-start.3
  15.3 2.2 %shard_map.66 = (bf16[2,128,192]{2,1,0:T(8,128)(2,1)S(1)}, bf16[2,4,768,256]{3,2,1,0:T(8,128)(2,1)S(1)}) custom-call(s32[11]{0:T(128)S(1)} %stack.74.refs_0_, f32[2,4,4,128]{3,2,1,0:T(4,128)S(1)} %select_maximum_fusion.refs_1_, s32[4,2,32,640]{3,2,1,0:T(8,128)S(1)} %get-tuple-element.52.refs_2_), custom_call_target="tpu_custom_call" | custom-call | tf_op jit(solution)/shard_map/pallas_call | solution.py:455
  18.8 3.9 %collective-permute-done.2.refs_3_ = s32[2,32,640]{2,1,0:T(8,128)S(1)} collective-permute-done((s32[2,32,640]{2,1,0:T(8,128)S(1)}, s32[2,32,640]{2,1,0:T(8,128)S(1)}, u32[]{:S(2)}, u32[]{:S(2)}) %collective-permute-start.2) | collective-permute-done | bytes 163872 | tf_op jit(solution)/shard_map/ppermute | solution.py:508
  23.4 3.1 %collective-permute-start.8 = (s32[1,2,24,640]{3,2,1,0:T(8,128)S(1)}, s32[1,2,24,640]{3,2,1,0:T(8,128)S(1)}, u32[]{:S(2)}, u32[]{:S(2)}) collective-permute-start(s32[1,2,24,640]{3,2,1,0:T(8,128)S(1)} %get-tuple-element.60), channel_id=1, source_target_pairs={{0,2},{1,3},{2,0},{3,1},{4,6},{5,7},{6,4},{7,5},{8,10},{9,11},{10,... | collective-permute-start | bytes 368648 | tf_op jit(solution)/shard_map/ppermute | solution.py:508
  27.1 3.1 %collective-permute-done.8.refs_3_ = s32[1,2,24,640]{3,2,1,0:T(8,128)S(1)} collective-permute-done((s32[1,2,24,640]{3,2,1,0:T(8,128)S(1)}, s32[1,2,24,640]{3,2,1,0:T(8,128)S(1)}, u32[]{:S(2)}, u32[]{:S(2)}) %collective-permute-start.8) | collective-permute-done | bytes 122912 | tf_op jit(solution)/shard_map/ppermute | solution.py:508
  32.1 1.8 %collective-permute-start.15 = (s32[2,32,640]{2,1,0:T(8,128)S(1)}, s32[2,32,640]{2,1,0:T(8,128)S(1)}, u32[]{:S(2)}, u32[]{:S(2)}) collective-permute-start(s32[2,32,640]{2,1,0:T(8,128)S(1)} %get-tuple-element.109), channel_id=1, source_target_pairs={{0,17},{1,16},{2,19},{3,18},{4,21},{5,20},{6,23},{7,22},{8,25},{9,... | collective-permute-start | bytes 491528 | tf_op jit(solution)/shard_map/ppermute | solution.py:508
  35.2 1.5 collective-permute-done.5.refs_3_
  36.7 13.4 %shard_map.70 = (f32[4,64,256]{2,1,0:T(8,128)S(1)}, f32[2,64,1024]{2,1,0:T(8,128)S(1)}, f32[2,28,1024]{2,1,0:T(8,128)S(1)}, f32[2,28,1024]{2,1,0:T(8,128)S(1)}) custom-call(s32[11]{0:T(128)S(1)} %stack.74.refs_0_, f32[8,128]{1,0:T(8,128)S(1)} %get-tuple-element.56.refs_1_, f32[2,64,1280]{2,1,0:T(8,128)S(1)} %get-tuple-element.55.refs_5_.refs_2_, ...), custom_call_target="tpu_custom_call" | custom-call | flops 13891534848 | bytes 2097152 | tf_op jit(solution)/shard_map/pallas_call | solution.py:455
  50.0 1.8 %collective-permute-start.16 = (f32[2,28,1024]{2,1,0:T(8,128)S(1)}, f32[2,28,1024]{2,1,0:T(8,128)S(1)}, u32[]{:S(2)}, u32[]{:S(2)}) collective-permute-start(f32[2,28,1024]{2,1,0:T(8,128)S(1)} %get-tuple-element.65), channel_id=1, source_target_pairs={{0,2},{1,3},{2,0},{3,1},{4,6},{5,7},{6,4},{7,5},{8,10},{9,11},{10,... | collective-permute-start | bytes 688136 | tf_op jit(solution)/shard_map/ppermute | solution.py:508
  53.6 2.0 %collective-permute-start.18 = (s32[1,2,24,640]{3,2,1,0:T(8,128)S(1)}, s32[1,2,24,640]{3,2,1,0:T(8,128)S(1)}, u32[]{:S(2)}, u32[]{:S(2)}) collective-permute-start(s32[1,2,24,640]{3,2,1,0:T(8,128)S(1)} %get-tuple-element.67), channel_id=1, source_target_pairs={{0,2},{1,3},{2,0},{3,1},{4,6},{5,7},{6,4},{7,5},{8,10},{9,11},{10,... | collective-permute-start | bytes 368648 | tf_op jit(solution)/shard_map/ppermute | solution.py:508
  55.8 4.9 %collective-permute-done.18.refs_4_ = s32[1,2,24,640]{3,2,1,0:T(8,128)S(1)} collective-permute-done((s32[1,2,24,640]{3,2,1,0:T(8,128)S(1)}, s32[1,2,24,640]{3,2,1,0:T(8,128)S(1)}, u32[]{:S(2)}, u32[]{:S(2)}) %collective-permute-start.18) | collective-permute-done | bytes 122912 | tf_op jit(solution)/shard_map/ppermute | solution.py:508
  63.5 2.2 %collective-permute-start.29 = (s32[2,2,24,640]{3,2,1,0:T(8,128)S(1)}, s32[2,2,24,640]{3,2,1,0:T(8,128)S(1)}, u32[]{:S(2)}, u32[]{:S(2)}) collective-permute-start(s32[2,2,24,640]{3,2,1,0:T(8,128)S(1)} %get-tuple-element.81), channel_id=1, source_target_pairs={{0,2},{1,3},{2,0},{3,1},{4,6},{5,7},{6,4},{7,5},{8,10},{9,11},{10,... | collective-permute-start | bytes 737288 | tf_op jit(solution)/shard_map/ppermute | solution.py:508
  67.5 13.3 %shard_map.75 = (f32[4,64,256]{2,1,0:T(8,128)S(1)}, f32[2,64,1024]{2,1,0:T(8,128)S(1)}, f32[2,28,1024]{2,1,0:T(8,128)S(1)}, f32[2,28,1024]{2,1,0:T(8,128)S(1)}) custom-call(s32[11]{0:T(128)S(1)} %stack.74.refs_0_, f32[8,128]{1,0:T(8,128)S(1)} %get-tuple-element.70.refs_1_, f32[2,64,1024]{2,1,0:T(8,128)S(1)} %get-tuple-element.64.refs_1_.refs_2_, ...), custom_call_target="tpu_custom_call" | custom-call | flops 13891534848 | bytes 2097152 | tf_op jit(solution)/shard_map/pallas_call | solution.py:455
  82.5 2.0 %collective-permute-start.26 = (f32[2,28,1024]{2,1,0:T(8,128)S(1)}, f32[2,28,1024]{2,1,0:T(8,128)S(1)}, u32[]{:S(2)}, u32[]{:S(2)}) collective-permute-start(f32[2,28,1024]{2,1,0:T(8,128)S(1)} %get-tuple-element.78), channel_id=1, source_target_pairs={{0,2},{1,3},{2,0},{3,1},{4,6},{5,7},{6,4},{7,5},{8,10},{9,11},{10,... | collective-permute-start | bytes 688136 | tf_op jit(solution)/shard_map/ppermute | solution.py:508
  87.2 3.8 %collective-permute-done.26.refs_2_.refs_3_ = f32[2,28,1024]{2,1,0:T(8,128)S(1)} collective-permute-done((f32[2,28,1024]{2,1,0:T(8,128)S(1)}, f32[2,28,1024]{2,1,0:T(8,128)S(1)}, u32[]{:S(2)}, u32[]{:S(2)}) %collective-permute-start.26) | collective-permute-done | bytes 229408 | tf_op jit(solution)/shard_map/ppermute | solution.py:508
  91.9 2.1 %collective-permute-start.33 = (f32[2,120,128]{2,1,0:T(8,128)S(1)}, f32[2,120,128]{2,1,0:T(8,128)S(1)}, u32[]{:S(2)}, u32[]{:S(2)}) collective-permute-start(f32[2,120,128]{2,1,0:T(8,128)S(1)} %get-tuple-element.86), channel_id=1, source_target_pairs={{0,1},{1,0},{2,3},{3,2},{4,5},{5,4},{6,7},{7,6},{8,9},{9,8},{10,11... | collective-permute-start | bytes 368648 | tf_op jit(solution)/shard_map/ppermute | solution.py:508
  94.0 3.0 %collective-permute-done.33.refs_5_ = f32[2,120,128]{2,1,0:T(8,128)S(1)} collective-permute-done((f32[2,120,128]{2,1,0:T(8,128)S(1)}, f32[2,120,128]{2,1,0:T(8,128)S(1)}, u32[]{:S(2)}, u32[]{:S(2)}) %collective-permute-start.33) | collective-permute-done | bytes 122912 | tf_op jit(solution)/shard_map/ppermute | solution.py:508
  97.0 13.5 %shard_map.80 = (f32[4,64,256]{2,1,0:T(8,128)S(1)}, f32[2,64,1024]{2,1,0:T(8,128)S(1)}, f32[2,28,1024]{2,1,0:T(8,128)S(1)}, f32[2,28,1024]{2,1,0:T(8,128)S(1)}) custom-call(s32[11]{0:T(128)S(1)} %stack.74.refs_0_, f32[8,128]{1,0:T(8,128)S(1)} %get-tuple-element.85.refs_1_, f32[2,64,1024]{2,1,0:T(8,128)S(1)} %get-tuple-element.77.refs_1_.refs_2_, ...), custom_call_target="tpu_custom_call" | custom-call | flops 13891534848 | bytes 2097152 | tf_op jit(solution)/shard_map/pallas_call | solution.py:455
  110.6 1.8 %collective-permute-start.36 = (f32[2,28,1024]{2,1,0:T(8,128)S(1)}, f32[2,28,1024]{2,1,0:T(8,128)S(1)}, u32[]{:S(2)}, u32[]{:S(2)}) collective-permute-start(f32[2,28,1024]{2,1,0:T(8,128)S(1)} %get-tuple-element.90), channel_id=1, source_target_pairs={{0,2},{1,3},{2,0},{3,1},{4,6},{5,7},{6,4},{7,5},{8,10},{9,11},{10,... | collective-permute-start | bytes 688136 | tf_op jit(solution)/shard_map/ppermute | solution.py:508
  112.4 5.4 %collective-permute-done.36.refs_2_.refs_3_ = f32[2,28,1024]{2,1,0:T(8,128)S(1)} collective-permute-done((f32[2,28,1024]{2,1,0:T(8,128)S(1)}, f32[2,28,1024]{2,1,0:T(8,128)S(1)}, u32[]{:S(2)}, u32[]{:S(2)}) %collective-permute-start.36) | collective-permute-done | bytes 229408 | tf_op jit(solution)/shard_map/ppermute | solution.py:508
  118.6 1.5 collective-permute-start.38
  121.1 2.4 %collective-permute-done.38.refs_5_ = f32[2,120,128]{2,1,0:T(8,128)S(1)} collective-permute-done((f32[2,120,128]{2,1,0:T(8,128)S(1)}, f32[2,120,128]{2,1,0:T(8,128)S(1)}, u32[]{:S(2)}, u32[]{:S(2)}) %collective-permute-start.38) | collective-permute-done | bytes 122912 | tf_op jit(solution)/shard_map/ppermute | solution.py:508
  123.6 12.9 %shard_map.82 = f32[4,64,256]{2,1,0:T(8,128)S(1)} custom-call(s32[11]{0:T(128)S(1)} %stack.74.refs_0_, f32[8,128]{1,0:T(8,128)S(1)} %get-tuple-element.92.refs_1_, f32[2,64,1024]{2,1,0:T(8,128)S(1)} %get-tuple-element.89.refs_1_.refs_2_, f32[2,28,1024]{2,1,0:T(8,128)S(1)} %collective-permute-done.36.refs_2_.refs_3_, ...), custom_call_target="tpu_custom_call" | custom-call | flops 13891534848 | bytes 2097152 | tf_op jit(solution)/shard_map/pallas_call | solution.py:455
  136.6 1.5 collective-permute-done.40
  138.3 2.0 %collective-permute-start.41 = (f32[4,32,256]{2,1,0:T(8,128)S(1)}, f32[4,32,256]{2,1,0:T(8,128)S(1)}, u32[]{:S(2)}, u32[]{:S(2)}) collective-permute-start(f32[4,32,256]{2,1,0:T(8,128)S(1)} %get-tuple-element.118), channel_id=1, source_target_pairs={{0,16},{1,17},{2,18},{3,19},{4,20},{5,21},{6,22},{7,23},{8,24},{9,... | collective-permute-start | bytes 393224 | tf_op jit(solution)/shard_map/ppermute | solution.py:508
  140.3 1.5 %collective-permute-start.43 = (f32[4,32,256]{2,1,0:T(8,128)S(1)}, f32[4,32,256]{2,1,0:T(8,128)S(1)}, u32[]{:S(2)}, u32[]{:S(2)}) collective-permute-start(f32[4,32,256]{2,1,0:T(8,128)S(1)} %get-tuple-element.117), channel_id=1, source_target_pairs={{0,17},{1,16},{2,19},{3,18},{4,21},{5,20},{6,23},{7,22},{8,25},{9,... | collective-permute-start | bytes 393224 | tf_op jit(solution)/shard_map/ppermute | solution.py:508
  142.4 1.8 %collective-permute-done.41 = f32[4,32,256]{2,1,0:T(8,128)S(1)} collective-permute-done((f32[4,32,256]{2,1,0:T(8,128)S(1)}, f32[4,32,256]{2,1,0:T(8,128)S(1)}, u32[]{:S(2)}, u32[]{:S(2)}) %collective-permute-start.41) | collective-permute-done | bytes 131104 | tf_op jit(solution)/shard_map/ppermute | solution.py:508
  144.2 4.3 %collective-permute-done.43 = f32[4,32,256]{2,1,0:T(8,128)S(1)} collective-permute-done((f32[4,32,256]{2,1,0:T(8,128)S(1)}, f32[4,32,256]{2,1,0:T(8,128)S(1)}, u32[]{:S(2)}, u32[]{:S(2)}) %collective-permute-start.43) | collective-permute-done | bytes 131104 | tf_op jit(solution)/shard_map/ppermute | solution.py:508
  148.5 1.5 collective-permute-done.42
  (107 shorter events, 28.5 us)
Async XLA Ops:
  3.4 14.2 %collective-permute-start.4 = (f32[2,32,1280]{2,1,0:T(8,128)S(1)}, f32[2,32,1280]{2,1,0:T(8,128)S(1)}, u32[]{:S(2)}, u32[]{:S(2)}) collective-permute-start(f32[2,32,1280]{2,1,0:T(8,128)S(1)} %get-tuple-element.50.refs_3_), channel_id=1, source_target_pairs={{0,1},{1,0},{2,3},{3,2},{4,5},{5,4},{6,7},{7,6},{8,9},{9,8},{10,11... | collective-permute-start | bytes 983048 | tf_op jit(solution)/shard_map/ppermute | solution.py:508
  11.7 7.2 %collective-permute-start.1 = (s32[2,32,640]{2,1,0:T(8,128)S(1)}, s32[2,32,640]{2,1,0:T(8,128)S(1)}, u32[]{:S(2)}, u32[]{:S(2)}) collective-permute-start(s32[2,32,640]{2,1,0:T(8,128)S(1)} %get-tuple-element.115), channel_id=1, source_target_pairs={{0,16},{1,17},{2,18},{3,19},{4,20},{5,21},{6,22},{7,23},{8,24},{9,... | collective-permute-start | bytes 491528 | tf_op jit(solution)/shard_map/ppermute | solution.py:508
  13.2 9.5 %collective-permute-start.2 = (s32[2,32,640]{2,1,0:T(8,128)S(1)}, s32[2,32,640]{2,1,0:T(8,128)S(1)}, u32[]{:S(2)}, u32[]{:S(2)}) collective-permute-start(s32[2,32,640]{2,1,0:T(8,128)S(1)} %get-tuple-element.114), channel_id=1, source_target_pairs={{0,1},{1,0},{2,3},{3,2},{4,5},{5,4},{6,7},{7,6},{8,9},{9,8},{10,11... | collective-permute-start | bytes 491528 | tf_op jit(solution)/shard_map/ppermute | solution.py:508
  13.7 9.0 %collective-permute-start.3 = (s32[2,32,640]{2,1,0:T(8,128)S(1)}, s32[2,32,640]{2,1,0:T(8,128)S(1)}, u32[]{:S(2)}, u32[]{:S(2)}) collective-permute-start(s32[2,32,640]{2,1,0:T(8,128)S(1)} %get-tuple-element.113), channel_id=1, source_target_pairs={{0,17},{1,16},{2,19},{3,18},{4,21},{5,20},{6,23},{7,22},{8,25},{9,... | collective-permute-start | bytes 491528 | tf_op jit(solution)/shard_map/ppermute | solution.py:508
  23.4 6.9 %collective-permute-start.8 = (s32[1,2,24,640]{3,2,1,0:T(8,128)S(1)}, s32[1,2,24,640]{3,2,1,0:T(8,128)S(1)}, u32[]{:S(2)}, u32[]{:S(2)}) collective-permute-start(s32[1,2,24,640]{3,2,1,0:T(8,128)S(1)} %get-tuple-element.60), channel_id=1, source_target_pairs={{0,2},{1,3},{2,0},{3,1},{4,6},{5,7},{6,4},{7,5},{8,10},{9,11},{10,... | collective-permute-start | bytes 368648 | tf_op jit(solution)/shard_map/ppermute | solution.py:508
  26.5 5.6 %collective-permute-start.7 = (s32[1,2,64,640]{3,2,1,0:T(8,128)S(1)}, s32[1,2,64,640]{3,2,1,0:T(8,128)S(1)}, u32[]{:S(2)}, u32[]{:S(2)}) collective-permute-start(s32[1,2,64,640]{3,2,1,0:T(8,128)S(1)} %get-tuple-element.59.refs_1_), channel_id=1, source_target_pairs={{0,8},{1,9},{2,10},{3,11},{4,12},{5,13},{6,14},{7,15},{8,0},{9,1},... | collective-permute-start | bytes 983048 | tf_op jit(solution)/shard_map/ppermute | solution.py:508
  26.5 10.1 %collective-permute-start.5 = (f32[2,28,1280]{2,1,0:T(8,128)S(1)}, f32[2,28,1280]{2,1,0:T(8,128)S(1)}, u32[]{:S(2)}, u32[]{:S(2)}) collective-permute-start(f32[2,28,1280]{2,1,0:T(8,128)S(1)} %get-tuple-element.57), channel_id=1, source_target_pairs={{0,2},{1,3},{2,0},{3,1},{4,6},{5,7},{6,4},{7,5},{8,10},{9,11},{10,... | collective-permute-start | bytes 860168 | tf_op jit(solution)/shard_map/ppermute | solution.py:508
  26.6 10.1 %collective-permute-start.6 = (f32[2,28,1280]{2,1,0:T(8,128)S(1)}, f32[2,28,1280]{2,1,0:T(8,128)S(1)}, u32[]{:S(2)}, u32[]{:S(2)}) collective-permute-start(f32[2,28,1280]{2,1,0:T(8,128)S(1)} %get-tuple-element.58), channel_id=1, source_target_pairs={{0,8},{1,9},{2,4},{3,5},{4,2},{5,3},{6,14},{7,15},{8,0},{9,1},{10,... | collective-permute-start | bytes 860168 | tf_op jit(solution)/shard_map/ppermute | solution.py:508
  30.3 21.6 %collective-permute-start.13 = (s32[2,32,640]{2,1,0:T(8,128)S(1)}, s32[2,32,640]{2,1,0:T(8,128)S(1)}, u32[]{:S(2)}, u32[]{:S(2)}) collective-permute-start(s32[2,32,640]{2,1,0:T(8,128)S(1)} %get-tuple-element.111), channel_id=1, source_target_pairs={{0,16},{1,17},{2,18},{3,19},{4,20},{5,21},{6,22},{7,23},{8,24},{9,... | collective-permute-start | bytes 491528 | tf_op jit(solution)/shard_map/ppermute | solution.py:508
  31.6 20.3 %collective-permute-start.14 = (s32[2,32,640]{2,1,0:T(8,128)S(1)}, s32[2,32,640]{2,1,0:T(8,128)S(1)}, u32[]{:S(2)}, u32[]{:S(2)}) collective-permute-start(s32[2,32,640]{2,1,0:T(8,128)S(1)} %get-tuple-element.110), channel_id=1, source_target_pairs={{0,1},{1,0},{2,3},{3,2},{4,5},{5,4},{6,7},{7,6},{8,9},{9,8},{10,11... | collective-permute-start | bytes 491528 | tf_op jit(solution)/shard_map/ppermute | solution.py:508
  32.1 19.8 %collective-permute-start.15 = (s32[2,32,640]{2,1,0:T(8,128)S(1)}, s32[2,32,640]{2,1,0:T(8,128)S(1)}, u32[]{:S(2)}, u32[]{:S(2)}) collective-permute-start(s32[2,32,640]{2,1,0:T(8,128)S(1)} %get-tuple-element.109), channel_id=1, source_target_pairs={{0,17},{1,16},{2,19},{3,18},{4,21},{5,20},{6,23},{7,22},{8,25},{9,... | collective-permute-start | bytes 491528 | tf_op jit(solution)/shard_map/ppermute | solution.py:508
  50.0 10.6 %collective-permute-start.16 = (f32[2,28,1024]{2,1,0:T(8,128)S(1)}, f32[2,28,1024]{2,1,0:T(8,128)S(1)}, u32[]{:S(2)}, u32[]{:S(2)}) collective-permute-start(f32[2,28,1024]{2,1,0:T(8,128)S(1)} %get-tuple-element.65), channel_id=1, source_target_pairs={{0,2},{1,3},{2,0},{3,1},{4,6},{5,7},{6,4},{7,5},{8,10},{9,11},{10,... | collective-permute-start | bytes 688136 | tf_op jit(solution)/shard_map/ppermute | solution.py:508
  51.9 8.8 %collective-permute-start.17 = (f32[2,28,1024]{2,1,0:T(8,128)S(1)}, f32[2,28,1024]{2,1,0:T(8,128)S(1)}, u32[]{:S(2)}, u32[]{:S(2)}) collective-permute-start(f32[2,28,1024]{2,1,0:T(8,128)S(1)} %get-tuple-element.66), channel_id=1, source_target_pairs={{0,8},{1,9},{2,4},{3,5},{4,2},{5,3},{6,14},{7,15},{8,0},{9,1},{10,... | collective-permute-start | bytes 688136 | tf_op jit(solution)/shard_map/ppermute | solution.py:508
  53.1 10.4 %collective-permute-start.22 = (s32[1,2,64,640]{3,2,1,0:T(8,128)S(1)}, s32[1,2,64,640]{3,2,1,0:T(8,128)S(1)}, u32[]{:S(2)}, u32[]{:S(2)}) collective-permute-start(s32[1,2,64,640]{3,2,1,0:T(8,128)S(1)} %get-tuple-element.73.refs_1_), channel_id=1, source_target_pairs={{0,8},{1,9},{2,10},{3,11},{4,12},{5,13},{6,14},{7,15},{8,0},{9,1},... | collective-permute-start | bytes 983048 | tf_op jit(solution)/shard_map/ppermute | solution.py:508
  53.6 7.1 %collective-permute-start.18 = (s32[1,2,24,640]{3,2,1,0:T(8,128)S(1)}, s32[1,2,24,640]{3,2,1,0:T(8,128)S(1)}, u32[]{:S(2)}, u32[]{:S(2)}) collective-permute-start(s32[1,2,24,640]{3,2,1,0:T(8,128)S(1)} %get-tuple-element.67), channel_id=1, source_target_pairs={{0,2},{1,3},{2,0},{3,1},{4,6},{5,7},{6,4},{7,5},{8,10},{9,11},{10,... | collective-permute-start | bytes 368648 | tf_op jit(solution)/shard_map/ppermute | solution.py:508
  55.6 5.1 %collective-permute-start.19 = (s32[1,2,24,640]{3,2,1,0:T(8,128)S(1)}, s32[1,2,24,640]{3,2,1,0:T(8,128)S(1)}, u32[]{:S(2)}, u32[]{:S(2)}) collective-permute-start(s32[1,2,24,640]{3,2,1,0:T(8,128)S(1)} %get-tuple-element.68), channel_id=1, source_target_pairs={{0,8},{1,9},{2,4},{3,5},{4,2},{5,3},{6,14},{7,15},{8,0},{9,1},{10,... | collective-permute-start | bytes 368648 | tf_op jit(solution)/shard_map/ppermute | solution.py:508
  62.1 5.4 %collective-permute-start.20 = (f32[2,120,128]{2,1,0:T(8,128)S(1)}, f32[2,120,128]{2,1,0:T(8,128)S(1)}, u32[]{:S(2)}, u32[]{:S(2)}) collective-permute-start(f32[2,120,128]{2,1,0:T(8,128)S(1)} %get-tuple-element.71), channel_id=1, source_target_pairs={{0,1},{1,0},{2,3},{3,2},{4,5},{5,4},{6,7},{7,6},{8,9},{9,8},{10,11... | collective-permute-start | bytes 368648 | tf_op jit(solution)/shard_map/ppermute | solution.py:508
  63.5 17.4 %collective-permute-start.29 = (s32[2,2,24,640]{3,2,1,0:T(8,128)S(1)}, s32[2,2,24,640]{3,2,1,0:T(8,128)S(1)}, u32[]{:S(2)}, u32[]{:S(2)}) collective-permute-start(s32[2,2,24,640]{3,2,1,0:T(8,128)S(1)} %get-tuple-element.81), channel_id=1, source_target_pairs={{0,2},{1,3},{2,0},{3,1},{4,6},{5,7},{6,4},{7,5},{8,10},{9,11},{10,... | collective-permute-start | bytes 737288 | tf_op jit(solution)/shard_map/ppermute | solution.py:508
  65.7 15.2 %collective-permute-start.30 = (s32[2,2,24,640]{3,2,1,0:T(8,128)S(1)}, s32[2,2,24,640]{3,2,1,0:T(8,128)S(1)}, u32[]{:S(2)}, u32[]{:S(2)}) collective-permute-start(s32[2,2,24,640]{3,2,1,0:T(8,128)S(1)} %get-tuple-element.82), channel_id=1, source_target_pairs={{0,8},{1,9},{2,4},{3,5},{4,2},{5,3},{6,14},{7,15},{8,0},{9,1},{10,... | collective-permute-start | bytes 737288 | tf_op jit(solution)/shard_map/ppermute | solution.py:508
  65.9 18.7 %collective-permute-start.28 = (s32[2,2,64,640]{3,2,1,0:T(8,128)S(1)}, s32[2,2,64,640]{3,2,1,0:T(8,128)S(1)}, u32[]{:S(2)}, u32[]{:S(2)}) collective-permute-start(s32[2,2,64,640]{3,2,1,0:T(8,128)S(1)} %get-tuple-element.80.refs_1_), channel_id=1, source_target_pairs={{0,8},{1,9},{2,10},{3,11},{4,12},{5,13},{6,14},{7,15},{8,0},{9,1},... | collective-permute-start | bytes 1966088 | tf_op jit(solution)/shard_map/ppermute | solution.py:508
  82.5 8.5 %collective-permute-start.26 = (f32[2,28,1024]{2,1,0:T(8,128)S(1)}, f32[2,28,1024]{2,1,0:T(8,128)S(1)}, u32[]{:S(2)}, u32[]{:S(2)}) collective-permute-start(f32[2,28,1024]{2,1,0:T(8,128)S(1)} %get-tuple-element.78), channel_id=1, source_target_pairs={{0,2},{1,3},{2,0},{3,1},{4,6},{5,7},{6,4},{7,5},{8,10},{9,11},{10,... | collective-permute-start | bytes 688136 | tf_op jit(solution)/shard_map/ppermute | solution.py:508
  84.6 6.5 %collective-permute-start.27 = (f32[2,28,1024]{2,1,0:T(8,128)S(1)}, f32[2,28,1024]{2,1,0:T(8,128)S(1)}, u32[]{:S(2)}, u32[]{:S(2)}) collective-permute-start(f32[2,28,1024]{2,1,0:T(8,128)S(1)} %get-tuple-element.79), channel_id=1, source_target_pairs={{0,8},{1,9},{2,4},{3,5},{4,2},{5,3},{6,14},{7,15},{8,0},{9,1},{10,... | collective-permute-start | bytes 688136 | tf_op jit(solution)/shard_map/ppermute | solution.py:508
  91.9 5.1 %collective-permute-start.33 = (f32[2,120,128]{2,1,0:T(8,128)S(1)}, f32[2,120,128]{2,1,0:T(8,128)S(1)}, u32[]{:S(2)}, u32[]{:S(2)}) collective-permute-start(f32[2,120,128]{2,1,0:T(8,128)S(1)} %get-tuple-element.86), channel_id=1, source_target_pairs={{0,1},{1,0},{2,3},{3,2},{4,5},{5,4},{6,7},{7,6},{8,9},{9,8},{10,11... | collective-permute-start | bytes 368648 | tf_op jit(solution)/shard_map/ppermute | solution.py:508
  110.6 7.2 %collective-permute-start.36 = (f32[2,28,1024]{2,1,0:T(8,128)S(1)}, f32[2,28,1024]{2,1,0:T(8,128)S(1)}, u32[]{:S(2)}, u32[]{:S(2)}) collective-permute-start(f32[2,28,1024]{2,1,0:T(8,128)S(1)} %get-tuple-element.90), channel_id=1, source_target_pairs={{0,2},{1,3},{2,0},{3,1},{4,6},{5,7},{6,4},{7,5},{8,10},{9,11},{10,... | collective-permute-start | bytes 688136 | tf_op jit(solution)/shard_map/ppermute | solution.py:508
  112.4 5.4 %collective-permute-start.37 = (f32[2,28,1024]{2,1,0:T(8,128)S(1)}, f32[2,28,1024]{2,1,0:T(8,128)S(1)}, u32[]{:S(2)}, u32[]{:S(2)}) collective-permute-start(f32[2,28,1024]{2,1,0:T(8,128)S(1)} %get-tuple-element.91), channel_id=1, source_target_pairs={{0,8},{1,9},{2,4},{3,5},{4,2},{5,3},{6,14},{7,15},{8,0},{9,1},{10,... | collective-permute-start | bytes 688136 | tf_op jit(solution)/shard_map/ppermute | solution.py:508
  118.6 4.9 %collective-permute-start.38 = (f32[2,120,128]{2,1,0:T(8,128)S(1)}, f32[2,120,128]{2,1,0:T(8,128)S(1)}, u32[]{:S(2)}, u32[]{:S(2)}) collective-permute-start(f32[2,120,128]{2,1,0:T(8,128)S(1)} %get-tuple-element.93), channel_id=1, source_target_pairs={{0,1},{1,0},{2,3},{3,2},{4,5},{5,4},{6,7},{7,6},{8,9},{9,8},{10,11... | collective-permute-start | bytes 368648 | tf_op jit(solution)/shard_map/ppermute | solution.py:508
  120.1 16.5 %collective-permute-start.12 = (f32[4,64,256]{2,1,0:T(8,128)S(1)}, f32[4,64,256]{2,1,0:T(8,128)S(1)}, u32[]{:S(2)}, u32[]{:S(2)}) collective-permute-start(f32[4,64,256]{2,1,0:T(8,128)S(1)} %get-tuple-element.63.refs_5_), channel_id=1, source_target_pairs={{0,8},{1,9},{2,10},{3,11},{4,12},{5,13},{6,14},{7,15},{8,0},{9,1},... | collective-permute-start | bytes 786440 | tf_op jit(solution)/shard_map/ppermute | solution.py:508
  120.6 16.0 %collective-permute-start.25 = (f32[4,64,256]{2,1,0:T(8,128)S(1)}, f32[4,64,256]{2,1,0:T(8,128)S(1)}, u32[]{:S(2)}, u32[]{:S(2)}) collective-permute-start(f32[4,64,256]{2,1,0:T(8,128)S(1)} %get-tuple-element.76.refs_1_), channel_id=1, source_target_pairs={{0,8},{1,9},{2,10},{3,11},{4,12},{5,13},{6,14},{7,15},{8,0},{9,1},... | collective-permute-start | bytes 786440 | tf_op jit(solution)/shard_map/ppermute | solution.py:508
  120.6 16.0 %collective-permute-start.35 = (f32[4,64,256]{2,1,0:T(8,128)S(1)}, f32[4,64,256]{2,1,0:T(8,128)S(1)}, u32[]{:S(2)}, u32[]{:S(2)}) collective-permute-start(f32[4,64,256]{2,1,0:T(8,128)S(1)} %get-tuple-element.88), channel_id=1, source_target_pairs={{0,8},{1,9},{2,10},{3,11},{4,12},{5,13},{6,14},{7,15},{8,0},{9,1},... | collective-permute-start | bytes 786440 | tf_op jit(solution)/shard_map/ppermute | solution.py:508
  138.3 5.9 %collective-permute-start.41 = (f32[4,32,256]{2,1,0:T(8,128)S(1)}, f32[4,32,256]{2,1,0:T(8,128)S(1)}, u32[]{:S(2)}, u32[]{:S(2)}) collective-permute-start(f32[4,32,256]{2,1,0:T(8,128)S(1)} %get-tuple-element.118), channel_id=1, source_target_pairs={{0,16},{1,17},{2,18},{3,19},{4,20},{5,21},{6,22},{7,23},{8,24},{9,... | collective-permute-start | bytes 393224 | tf_op jit(solution)/shard_map/ppermute | solution.py:508
  140.3 8.2 %collective-permute-start.43 = (f32[4,32,256]{2,1,0:T(8,128)S(1)}, f32[4,32,256]{2,1,0:T(8,128)S(1)}, u32[]{:S(2)}, u32[]{:S(2)}) collective-permute-start(f32[4,32,256]{2,1,0:T(8,128)S(1)} %get-tuple-element.117), channel_id=1, source_target_pairs={{0,17},{1,16},{2,19},{3,18},{4,21},{5,20},{6,23},{7,22},{8,25},{9,... | collective-permute-start | bytes 393224 | tf_op jit(solution)/shard_map/ppermute | solution.py:508
  141.9 8.1 %collective-permute-start.42 = (f32[4,32,256]{2,1,0:T(8,128)S(1)}, f32[4,32,256]{2,1,0:T(8,128)S(1)}, u32[]{:S(2)}, u32[]{:S(2)}) collective-permute-start(f32[4,32,256]{2,1,0:T(8,128)S(1)} %constant_dynamic-slice_fusion.1), channel_id=1, source_target_pairs={{0,1},{1,0},{2,3},{3,2},{4,5},{5,4},{6,7},{7,6},{8,9},{9,8},{10,11... | collective-permute-start | bytes 393224 | tf_op jit(solution)/shard_map/ppermute | solution.py:508
  (18 other events, 60.3 us)

commit v3 on v2

--- a/solution.py
+++ b/solution.py
@@ -396,6 +396,8 @@
                 s = acc[k * each + b]
                 q = acc[k * each + windows + b]
                 im_ref[l, r, b * LANES : (b + 1) * LANES] = s[0] * q[0] - s[1] * q[1]
+            if last and l == levels - 1:
+                continue
             for f in range(2):
                 for b in range(windows):
                     at = (f * windows + b) * LANES

time: 151 us -> 151 us (level)
  no operation moved by 1% of the time
where the time goes in v3:
time: 151 us
  Pallas kernels  69.7 us (46%)
  waiting for transfers between devices  39.4 us (26%)
  starting transfers between devices  34.8 us (23%)
  local copies, waits for them, and re-layouts  4.77 us (3%)
  other arithmetic  1.77 us (1%)
    pallas_call x19, Pallas kernels, call(): pl.pallas_call(run, in_specs=[pl.BlockSpec(memory_space=pltpu.SMEM)] + ne...  69.7 us
    ppermute x44, waiting for transfers between devices, move(): return lax.ppermute(x, AXES, pairs)  39.4 us
    ppermute x44, starting transfers between devices, move(): return lax.ppermute(x, AXES, pairs)  34.8 us
    unnamed x12, local copies, waits for them, and re-layouts  4.54 us
  transfers between devices with their start and end apart: 44, of which 14 were waited for; matrix products, arithmetic and copies ran while one was open for 1% of the time, Pallas kernels for 35%

profile of v3, /device:TPU:0, one launch (start us, length us, event | category | flops | bytes accessed | tf_op | source)
XLA Modules:
  0.0 150.9 jit_solution(13513850134311464245)
XLA Ops:
  3.4 3.0 %collective-permute-start.4 = (f32[2,32,1280]{2,1,0:T(8,128)S(1)}, f32[2,32,1280]{2,1,0:T(8,128)S(1)}, u32[]{:S(2)}, u32[]{:S(2)}) collective-permute-start(f32[2,32,1280]{2,1,0:T(8,128)S(1)} %get-tuple-element.50.refs_3_), channel_id=1, source_target_pairs={{0,1},{1,0},{2,3},{3,2},{4,5},{5,4},{6,7},{7,6},{8,9},{9,8},{10,11... | collective-permute-start | bytes 983048 | tf_op jit(solution)/shard_map/ppermute | solution.py:510
  9.9 1.5 %collective-permute-done = s32[4,2,32,640]{3,2,1,0:T(8,128)S(1)} collective-permute-done((s32[4,2,32,640]{3,2,1,0:T(8,128)S(1)}, s32[4,2,32,640]{3,2,1,0:T(8,128)S(1)}, u32[]{:S(2)}, u32[]{:S(2)}) %collective-permute-start) | collective-permute-done | bytes 655392 | tf_op jit(solution)/shard_map/ppermute | solution.py:510
  11.7 1.6 %collective-permute-start.1 = (s32[2,32,640]{2,1,0:T(8,128)S(1)}, s32[2,32,640]{2,1,0:T(8,128)S(1)}, u32[]{:S(2)}, u32[]{:S(2)}) collective-permute-start(s32[2,32,640]{2,1,0:T(8,128)S(1)} %get-tuple-element.115), channel_id=1, source_target_pairs={{0,16},{1,17},{2,18},{3,19},{4,20},{5,21},{6,22},{7,23},{8,24},{9,... | collective-permute-start | bytes 491528 | tf_op jit(solution)/shard_map/ppermute | solution.py:510
  13.7 1.5 collective-permute-start.3
  15.3 2.2 %shard_map.66 = (bf16[2,128,192]{2,1,0:T(8,128)(2,1)S(1)}, bf16[2,4,768,256]{3,2,1,0:T(8,128)(2,1)S(1)}) custom-call(s32[11]{0:T(128)S(1)} %stack.74.refs_0_, f32[2,4,4,128]{3,2,1,0:T(4,128)S(1)} %select_maximum_fusion.refs_1_, s32[4,2,32,640]{3,2,1,0:T(8,128)S(1)} %get-tuple-element.52.refs_2_), custom_call_target="tpu_custom_call" | custom-call | tf_op jit(solution)/shard_map/pallas_call | solution.py:457
  18.8 3.9 %collective-permute-done.2.refs_3_ = s32[2,32,640]{2,1,0:T(8,128)S(1)} collective-permute-done((s32[2,32,640]{2,1,0:T(8,128)S(1)}, s32[2,32,640]{2,1,0:T(8,128)S(1)}, u32[]{:S(2)}, u32[]{:S(2)}) %collective-permute-start.2) | collective-permute-done | bytes 163872 | tf_op jit(solution)/shard_map/ppermute | solution.py:510
  23.4 3.1 %collective-permute-start.8 = (s32[1,2,24,640]{3,2,1,0:T(8,128)S(1)}, s32[1,2,24,640]{3,2,1,0:T(8,128)S(1)}, u32[]{:S(2)}, u32[]{:S(2)}) collective-permute-start(s32[1,2,24,640]{3,2,1,0:T(8,128)S(1)} %get-tuple-element.60), channel_id=1, source_target_pairs={{0,2},{1,3},{2,0},{3,1},{4,6},{5,7},{6,4},{7,5},{8,10},{9,11},{10,... | collective-permute-start | bytes 368648 | tf_op jit(solution)/shard_map/ppermute | solution.py:510
  27.1 3.1 %collective-permute-done.8.refs_3_ = s32[1,2,24,640]{3,2,1,0:T(8,128)S(1)} collective-permute-done((s32[1,2,24,640]{3,2,1,0:T(8,128)S(1)}, s32[1,2,24,640]{3,2,1,0:T(8,128)S(1)}, u32[]{:S(2)}, u32[]{:S(2)}) %collective-permute-start.8) | collective-permute-done | bytes 122912 | tf_op jit(solution)/shard_map/ppermute | solution.py:510
  32.1 1.8 %collective-permute-start.15 = (s32[2,32,640]{2,1,0:T(8,128)S(1)}, s32[2,32,640]{2,1,0:T(8,128)S(1)}, u32[]{:S(2)}, u32[]{:S(2)}) collective-permute-start(s32[2,32,640]{2,1,0:T(8,128)S(1)} %get-tuple-element.109), channel_id=1, source_target_pairs={{0,17},{1,16},{2,19},{3,18},{4,21},{5,20},{6,23},{7,22},{8,25},{9,... | collective-permute-start | bytes 491528 | tf_op jit(solution)/shard_map/ppermute | solution.py:510
  35.2 1.5 collective-permute-done.5.refs_3_
  36.7 13.4 %shard_map.70 = (f32[4,64,256]{2,1,0:T(8,128)S(1)}, f32[2,64,1024]{2,1,0:T(8,128)S(1)}, f32[2,28,1024]{2,1,0:T(8,128)S(1)}, f32[2,28,1024]{2,1,0:T(8,128)S(1)}) custom-call(s32[11]{0:T(128)S(1)} %stack.74.refs_0_, f32[8,128]{1,0:T(8,128)S(1)} %get-tuple-element.56.refs_1_, f32[2,64,1280]{2,1,0:T(8,128)S(1)} %get-tuple-element.55.refs_5_.refs_2_, ...), custom_call_target="tpu_custom_call" | custom-call | flops 13891534848 | bytes 2097152 | tf_op jit(solution)/shard_map/pallas_call | solution.py:457
  50.0 1.8 %collective-permute-start.16 = (f32[2,28,1024]{2,1,0:T(8,128)S(1)}, f32[2,28,1024]{2,1,0:T(8,128)S(1)}, u32[]{:S(2)}, u32[]{:S(2)}) collective-permute-start(f32[2,28,1024]{2,1,0:T(8,128)S(1)} %get-tuple-element.65), channel_id=1, source_target_pairs={{0,2},{1,3},{2,0},{3,1},{4,6},{5,7},{6,4},{7,5},{8,10},{9,11},{10,... | collective-permute-start | bytes 688136 | tf_op jit(solution)/shard_map/ppermute | solution.py:510
  53.6 2.0 %collective-permute-start.18 = (s32[1,2,24,640]{3,2,1,0:T(8,128)S(1)}, s32[1,2,24,640]{3,2,1,0:T(8,128)S(1)}, u32[]{:S(2)}, u32[]{:S(2)}) collective-permute-start(s32[1,2,24,640]{3,2,1,0:T(8,128)S(1)} %get-tuple-element.67), channel_id=1, source_target_pairs={{0,2},{1,3},{2,0},{3,1},{4,6},{5,7},{6,4},{7,5},{8,10},{9,11},{10,... | collective-permute-start | bytes 368648 | tf_op jit(solution)/shard_map/ppermute | solution.py:510
  55.8 4.9 %collective-permute-done.18.refs_4_ = s32[1,2,24,640]{3,2,1,0:T(8,128)S(1)} collective-permute-done((s32[1,2,24,640]{3,2,1,0:T(8,128)S(1)}, s32[1,2,24,640]{3,2,1,0:T(8,128)S(1)}, u32[]{:S(2)}, u32[]{:S(2)}) %collective-permute-start.18) | collective-permute-done | bytes 122912 | tf_op jit(solution)/shard_map/ppermute | solution.py:510
  63.5 2.2 %collective-permute-start.29 = (s32[2,2,24,640]{3,2,1,0:T(8,128)S(1)}, s32[2,2,24,640]{3,2,1,0:T(8,128)S(1)}, u32[]{:S(2)}, u32[]{:S(2)}) collective-permute-start(s32[2,2,24,640]{3,2,1,0:T(8,128)S(1)} %get-tuple-element.81), channel_id=1, source_target_pairs={{0,2},{1,3},{2,0},{3,1},{4,6},{5,7},{6,4},{7,5},{8,10},{9,11},{10,... | collective-permute-start | bytes 737288 | tf_op jit(solution)/shard_map/ppermute | solution.py:510
  67.5 13.3 %shard_map.75 = (f32[4,64,256]{2,1,0:T(8,128)S(1)}, f32[2,64,1024]{2,1,0:T(8,128)S(1)}, f32[2,28,1024]{2,1,0:T(8,128)S(1)}, f32[2,28,1024]{2,1,0:T(8,128)S(1)}) custom-call(s32[11]{0:T(128)S(1)} %stack.74.refs_0_, f32[8,128]{1,0:T(8,128)S(1)} %get-tuple-element.70.refs_1_, f32[2,64,1024]{2,1,0:T(8,128)S(1)} %get-tuple-element.64.refs_1_.refs_2_, ...), custom_call_target="tpu_custom_call" | custom-call | flops 13891534848 | bytes 2097152 | tf_op jit(solution)/shard_map/pallas_call | solution.py:457
  82.5 2.0 %collective-permute-start.26 = (f32[2,28,1024]{2,1,0:T(8,128)S(1)}, f32[2,28,1024]{2,1,0:T(8,128)S(1)}, u32[]{:S(2)}, u32[]{:S(2)}) collective-permute-start(f32[2,28,1024]{2,1,0:T(8,128)S(1)} %get-tuple-element.78), channel_id=1, source_target_pairs={{0,2},{1,3},{2,0},{3,1},{4,6},{5,7},{6,4},{7,5},{8,10},{9,11},{10,... | collective-permute-start | bytes 688136 | tf_op jit(solution)/shard_map/ppermute | solution.py:510
  87.2 3.8 %collective-permute-done.26.refs_2_.refs_3_ = f32[2,28,1024]{2,1,0:T(8,128)S(1)} collective-permute-done((f32[2,28,1024]{2,1,0:T(8,128)S(1)}, f32[2,28,1024]{2,1,0:T(8,128)S(1)}, u32[]{:S(2)}, u32[]{:S(2)}) %collective-permute-start.26) | collective-permute-done | bytes 229408 | tf_op jit(solution)/shard_map/ppermute | solution.py:510
  91.9 2.1 %collective-permute-start.33 = (f32[2,120,128]{2,1,0:T(8,128)S(1)}, f32[2,120,128]{2,1,0:T(8,128)S(1)}, u32[]{:S(2)}, u32[]{:S(2)}) collective-permute-start(f32[2,120,128]{2,1,0:T(8,128)S(1)} %get-tuple-element.86), channel_id=1, source_target_pairs={{0,1},{1,0},{2,3},{3,2},{4,5},{5,4},{6,7},{7,6},{8,9},{9,8},{10,11... | collective-permute-start | bytes 368648 | tf_op jit(solution)/shard_map/ppermute | solution.py:510
  94.0 3.0 %collective-permute-done.33.refs_5_ = f32[2,120,128]{2,1,0:T(8,128)S(1)} collective-permute-done((f32[2,120,128]{2,1,0:T(8,128)S(1)}, f32[2,120,128]{2,1,0:T(8,128)S(1)}, u32[]{:S(2)}, u32[]{:S(2)}) %collective-permute-start.33) | collective-permute-done | bytes 122912 | tf_op jit(solution)/shard_map/ppermute | solution.py:510
  97.0 13.5 %shard_map.80 = (f32[4,64,256]{2,1,0:T(8,128)S(1)}, f32[2,64,1024]{2,1,0:T(8,128)S(1)}, f32[2,28,1024]{2,1,0:T(8,128)S(1)}, f32[2,28,1024]{2,1,0:T(8,128)S(1)}) custom-call(s32[11]{0:T(128)S(1)} %stack.74.refs_0_, f32[8,128]{1,0:T(8,128)S(1)} %get-tuple-element.85.refs_1_, f32[2,64,1024]{2,1,0:T(8,128)S(1)} %get-tuple-element.77.refs_1_.refs_2_, ...), custom_call_target="tpu_custom_call" | custom-call | flops 13891534848 | bytes 2097152 | tf_op jit(solution)/shard_map/pallas_call | solution.py:457
  110.6 1.8 %collective-permute-start.36 = (f32[2,28,1024]{2,1,0:T(8,128)S(1)}, f32[2,28,1024]{2,1,0:T(8,128)S(1)}, u32[]{:S(2)}, u32[]{:S(2)}) collective-permute-start(f32[2,28,1024]{2,1,0:T(8,128)S(1)} %get-tuple-element.90), channel_id=1, source_target_pairs={{0,2},{1,3},{2,0},{3,1},{4,6},{5,7},{6,4},{7,5},{8,10},{9,11},{10,... | collective-permute-start | bytes 688136 | tf_op jit(solution)/shard_map/ppermute | solution.py:510
  112.4 5.4 %collective-permute-done.36.refs_2_.refs_3_ = f32[2,28,1024]{2,1,0:T(8,128)S(1)} collective-permute-done((f32[2,28,1024]{2,1,0:T(8,128)S(1)}, f32[2,28,1024]{2,1,0:T(8,128)S(1)}, u32[]{:S(2)}, u32[]{:S(2)}) %collective-permute-start.36) | collective-permute-done | bytes 229408 | tf_op jit(solution)/shard_map/ppermute | solution.py:510
  118.6 1.5 collective-permute-start.38
  121.1 2.4 %collective-permute-done.38.refs_5_ = f32[2,120,128]{2,1,0:T(8,128)S(1)} collective-permute-done((f32[2,120,128]{2,1,0:T(8,128)S(1)}, f32[2,120,128]{2,1,0:T(8,128)S(1)}, u32[]{:S(2)}, u32[]{:S(2)}) %collective-permute-start.38) | collective-permute-done | bytes 122912 | tf_op jit(solution)/shard_map/ppermute | solution.py:510
  123.6 12.9 %shard_map.82 = f32[4,64,256]{2,1,0:T(8,128)S(1)} custom-call(s32[11]{0:T(128)S(1)} %stack.74.refs_0_, f32[8,128]{1,0:T(8,128)S(1)} %get-tuple-element.92.refs_1_, f32[2,64,1024]{2,1,0:T(8,128)S(1)} %get-tuple-element.89.refs_1_.refs_2_, f32[2,28,1024]{2,1,0:T(8,128)S(1)} %collective-permute-done.36.refs_2_.refs_3_, ...), custom_call_target="tpu_custom_call" | custom-call | flops 13891534848 | bytes 2097152 | tf_op jit(solution)/shard_map/pallas_call | solution.py:457
  136.5 1.5 collective-permute-done.40
  138.2 2.0 %collective-permute-start.41 = (f32[4,32,256]{2,1,0:T(8,128)S(1)}, f32[4,32,256]{2,1,0:T(8,128)S(1)}, u32[]{:S(2)}, u32[]{:S(2)}) collective-permute-start(f32[4,32,256]{2,1,0:T(8,128)S(1)} %get-tuple-element.118), channel_id=1, source_target_pairs={{0,16},{1,17},{2,18},{3,19},{4,20},{5,21},{6,22},{7,23},{8,24},{9,... | collective-permute-start | bytes 393224 | tf_op jit(solution)/shard_map/ppermute | solution.py:510
  140.3 1.5 %collective-permute-start.43 = (f32[4,32,256]{2,1,0:T(8,128)S(1)}, f32[4,32,256]{2,1,0:T(8,128)S(1)}, u32[]{:S(2)}, u32[]{:S(2)}) collective-permute-start(f32[4,32,256]{2,1,0:T(8,128)S(1)} %get-tuple-element.117), channel_id=1, source_target_pairs={{0,17},{1,16},{2,19},{3,18},{4,21},{5,20},{6,23},{7,22},{8,25},{9,... | collective-permute-start | bytes 393224 | tf_op jit(solution)/shard_map/ppermute | solution.py:510
  142.4 1.8 %collective-permute-done.41 = f32[4,32,256]{2,1,0:T(8,128)S(1)} collective-permute-done((f32[4,32,256]{2,1,0:T(8,128)S(1)}, f32[4,32,256]{2,1,0:T(8,128)S(1)}, u32[]{:S(2)}, u32[]{:S(2)}) %collective-permute-start.41) | collective-permute-done | bytes 131104 | tf_op jit(solution)/shard_map/ppermute | solution.py:510
  144.1 4.3 %collective-permute-done.43 = f32[4,32,256]{2,1,0:T(8,128)S(1)} collective-permute-done((f32[4,32,256]{2,1,0:T(8,128)S(1)}, f32[4,32,256]{2,1,0:T(8,128)S(1)}, u32[]{:S(2)}, u32[]{:S(2)}) %collective-permute-start.43) | collective-permute-done | bytes 131104 | tf_op jit(solution)/shard_map/ppermute | solution.py:510
  148.4 1.5 collective-permute-done.42
  (107 shorter events, 28.5 us)
Async XLA Ops:
  3.4 14.2 %collective-permute-start.4 = (f32[2,32,1280]{2,1,0:T(8,128)S(1)}, f32[2,32,1280]{2,1,0:T(8,128)S(1)}, u32[]{:S(2)}, u32[]{:S(2)}) collective-permute-start(f32[2,32,1280]{2,1,0:T(8,128)S(1)} %get-tuple-element.50.refs_3_), channel_id=1, source_target_pairs={{0,1},{1,0},{2,3},{3,2},{4,5},{5,4},{6,7},{7,6},{8,9},{9,8},{10,11... | collective-permute-start | bytes 983048 | tf_op jit(solution)/shard_map/ppermute | solution.py:510
  11.7 7.2 %collective-permute-start.1 = (s32[2,32,640]{2,1,0:T(8,128)S(1)}, s32[2,32,640]{2,1,0:T(8,128)S(1)}, u32[]{:S(2)}, u32[]{:S(2)}) collective-permute-start(s32[2,32,640]{2,1,0:T(8,128)S(1)} %get-tuple-element.115), channel_id=1, source_target_pairs={{0,16},{1,17},{2,18},{3,19},{4,20},{5,21},{6,22},{7,23},{8,24},{9,... | collective-permute-start | bytes 491528 | tf_op jit(solution)/shard_map/ppermute | solution.py:510
  13.2 9.5 %collective-permute-start.2 = (s32[2,32,640]{2,1,0:T(8,128)S(1)}, s32[2,32,640]{2,1,0:T(8,128)S(1)}, u32[]{:S(2)}, u32[]{:S(2)}) collective-permute-start(s32[2,32,640]{2,1,0:T(8,128)S(1)} %get-tuple-element.114), channel_id=1, source_target_pairs={{0,1},{1,0},{2,3},{3,2},{4,5},{5,4},{6,7},{7,6},{8,9},{9,8},{10,11... | collective-permute-start | bytes 491528 | tf_op jit(solution)/shard_map/ppermute | solution.py:510
  13.7 9.0 %collective-permute-start.3 = (s32[2,32,640]{2,1,0:T(8,128)S(1)}, s32[2,32,640]{2,1,0:T(8,128)S(1)}, u32[]{:S(2)}, u32[]{:S(2)}) collective-permute-start(s32[2,32,640]{2,1,0:T(8,128)S(1)} %get-tuple-element.113), channel_id=1, source_target_pairs={{0,17},{1,16},{2,19},{3,18},{4,21},{5,20},{6,23},{7,22},{8,25},{9,... | collective-permute-start | bytes 491528 | tf_op jit(solution)/shard_map/ppermute | solution.py:510
  23.4 6.9 %collective-permute-start.8 = (s32[1,2,24,640]{3,2,1,0:T(8,128)S(1)}, s32[1,2,24,640]{3,2,1,0:T(8,128)S(1)}, u32[]{:S(2)}, u32[]{:S(2)}) collective-permute-start(s32[1,2,24,640]{3,2,1,0:T(8,128)S(1)} %get-tuple-element.60), channel_id=1, source_target_pairs={{0,2},{1,3},{2,0},{3,1},{4,6},{5,7},{6,4},{7,5},{8,10},{9,11},{10,... | collective-permute-start | bytes 368648 | tf_op jit(solution)/shard_map/ppermute | solution.py:510
  26.5 5.6 %collective-permute-start.7 = (s32[1,2,64,640]{3,2,1,0:T(8,128)S(1)}, s32[1,2,64,640]{3,2,1,0:T(8,128)S(1)}, u32[]{:S(2)}, u32[]{:S(2)}) collective-permute-start(s32[1,2,64,640]{3,2,1,0:T(8,128)S(1)} %get-tuple-element.59.refs_1_), channel_id=1, source_target_pairs={{0,8},{1,9},{2,10},{3,11},{4,12},{5,13},{6,14},{7,15},{8,0},{9,1},... | collective-permute-start | bytes 983048 | tf_op jit(solution)/shard_map/ppermute | solution.py:510
  26.5 10.1 %collective-permute-start.5 = (f32[2,28,1280]{2,1,0:T(8,128)S(1)}, f32[2,28,1280]{2,1,0:T(8,128)S(1)}, u32[]{:S(2)}, u32[]{:S(2)}) collective-permute-start(f32[2,28,1280]{2,1,0:T(8,128)S(1)} %get-tuple-element.57), channel_id=1, source_target_pairs={{0,2},{1,3},{2,0},{3,1},{4,6},{5,7},{6,4},{7,5},{8,10},{9,11},{10,... | collective-permute-start | bytes 860168 | tf_op jit(solution)/shard_map/ppermute | solution.py:510
  26.6 10.1 %collective-permute-start.6 = (f32[2,28,1280]{2,1,0:T(8,128)S(1)}, f32[2,28,1280]{2,1,0:T(8,128)S(1)}, u32[]{:S(2)}, u32[]{:S(2)}) collective-permute-start(f32[2,28,1280]{2,1,0:T(8,128)S(1)} %get-tuple-element.58), channel_id=1, source_target_pairs={{0,8},{1,9},{2,4},{3,5},{4,2},{5,3},{6,14},{7,15},{8,0},{9,1},{10,... | collective-permute-start | bytes 860168 | tf_op jit(solution)/shard_map/ppermute | solution.py:510
  30.3 21.6 %collective-permute-start.13 = (s32[2,32,640]{2,1,0:T(8,128)S(1)}, s32[2,32,640]{2,1,0:T(8,128)S(1)}, u32[]{:S(2)}, u32[]{:S(2)}) collective-permute-start(s32[2,32,640]{2,1,0:T(8,128)S(1)} %get-tuple-element.111), channel_id=1, source_target_pairs={{0,16},{1,17},{2,18},{3,19},{4,20},{5,21},{6,22},{7,23},{8,24},{9,... | collective-permute-start | bytes 491528 | tf_op jit(solution)/shard_map/ppermute | solution.py:510
  31.6 20.3 %collective-permute-start.14 = (s32[2,32,640]{2,1,0:T(8,128)S(1)}, s32[2,32,640]{2,1,0:T(8,128)S(1)}, u32[]{:S(2)}, u32[]{:S(2)}) collective-permute-start(s32[2,32,640]{2,1,0:T(8,128)S(1)} %get-tuple-element.110), channel_id=1, source_target_pairs={{0,1},{1,0},{2,3},{3,2},{4,5},{5,4},{6,7},{7,6},{8,9},{9,8},{10,11... | collective-permute-start | bytes 491528 | tf_op jit(solution)/shard_map/ppermute | solution.py:510
  32.1 19.8 %collective-permute-start.15 = (s32[2,32,640]{2,1,0:T(8,128)S(1)}, s32[2,32,640]{2,1,0:T(8,128)S(1)}, u32[]{:S(2)}, u32[]{:S(2)}) collective-permute-start(s32[2,32,640]{2,1,0:T(8,128)S(1)} %get-tuple-element.109), channel_id=1, source_target_pairs={{0,17},{1,16},{2,19},{3,18},{4,21},{5,20},{6,23},{7,22},{8,25},{9,... | collective-permute-start | bytes 491528 | tf_op jit(solution)/shard_map/ppermute | solution.py:510
  50.0 10.6 %collective-permute-start.16 = (f32[2,28,1024]{2,1,0:T(8,128)S(1)}, f32[2,28,1024]{2,1,0:T(8,128)S(1)}, u32[]{:S(2)}, u32[]{:S(2)}) collective-permute-start(f32[2,28,1024]{2,1,0:T(8,128)S(1)} %get-tuple-element.65), channel_id=1, source_target_pairs={{0,2},{1,3},{2,0},{3,1},{4,6},{5,7},{6,4},{7,5},{8,10},{9,11},{10,... | collective-permute-start | bytes 688136 | tf_op jit(solution)/shard_map/ppermute | solution.py:510
  51.9 8.8 %collective-permute-start.17 = (f32[2,28,1024]{2,1,0:T(8,128)S(1)}, f32[2,28,1024]{2,1,0:T(8,128)S(1)}, u32[]{:S(2)}, u32[]{:S(2)}) collective-permute-start(f32[2,28,1024]{2,1,0:T(8,128)S(1)} %get-tuple-element.66), channel_id=1, source_target_pairs={{0,8},{1,9},{2,4},{3,5},{4,2},{5,3},{6,14},{7,15},{8,0},{9,1},{10,... | collective-permute-start | bytes 688136 | tf_op jit(solution)/shard_map/ppermute | solution.py:510
  53.1 10.4 %collective-permute-start.22 = (s32[1,2,64,640]{3,2,1,0:T(8,128)S(1)}, s32[1,2,64,640]{3,2,1,0:T(8,128)S(1)}, u32[]{:S(2)}, u32[]{:S(2)}) collective-permute-start(s32[1,2,64,640]{3,2,1,0:T(8,128)S(1)} %get-tuple-element.73.refs_1_), channel_id=1, source_target_pairs={{0,8},{1,9},{2,10},{3,11},{4,12},{5,13},{6,14},{7,15},{8,0},{9,1},... | collective-permute-start | bytes 983048 | tf_op jit(solution)/shard_map/ppermute | solution.py:510
  53.6 7.1 %collective-permute-start.18 = (s32[1,2,24,640]{3,2,1,0:T(8,128)S(1)}, s32[1,2,24,640]{3,2,1,0:T(8,128)S(1)}, u32[]{:S(2)}, u32[]{:S(2)}) collective-permute-start(s32[1,2,24,640]{3,2,1,0:T(8,128)S(1)} %get-tuple-element.67), channel_id=1, source_target_pairs={{0,2},{1,3},{2,0},{3,1},{4,6},{5,7},{6,4},{7,5},{8,10},{9,11},{10,... | collective-permute-start | bytes 368648 | tf_op jit(solution)/shard_map/ppermute | solution.py:510
  55.6 5.1 %collective-permute-start.19 = (s32[1,2,24,640]{3,2,1,0:T(8,128)S(1)}, s32[1,2,24,640]{3,2,1,0:T(8,128)S(1)}, u32[]{:S(2)}, u32[]{:S(2)}) collective-permute-start(s32[1,2,24,640]{3,2,1,0:T(8,128)S(1)} %get-tuple-element.68), channel_id=1, source_target_pairs={{0,8},{1,9},{2,4},{3,5},{4,2},{5,3},{6,14},{7,15},{8,0},{9,1},{10,... | collective-permute-start | bytes 368648 | tf_op jit(solution)/shard_map/ppermute | solution.py:510
  62.1 5.4 %collective-permute-start.20 = (f32[2,120,128]{2,1,0:T(8,128)S(1)}, f32[2,120,128]{2,1,0:T(8,128)S(1)}, u32[]{:S(2)}, u32[]{:S(2)}) collective-permute-start(f32[2,120,128]{2,1,0:T(8,128)S(1)} %get-tuple-element.71), channel_id=1, source_target_pairs={{0,1},{1,0},{2,3},{3,2},{4,5},{5,4},{6,7},{7,6},{8,9},{9,8},{10,11... | collective-permute-start | bytes 368648 | tf_op jit(solution)/shard_map/ppermute | solution.py:510
  63.5 17.4 %collective-permute-start.29 = (s32[2,2,24,640]{3,2,1,0:T(8,128)S(1)}, s32[2,2,24,640]{3,2,1,0:T(8,128)S(1)}, u32[]{:S(2)}, u32[]{:S(2)}) collective-permute-start(s32[2,2,24,640]{3,2,1,0:T(8,128)S(1)} %get-tuple-element.81), channel_id=1, source_target_pairs={{0,2},{1,3},{2,0},{3,1},{4,6},{5,7},{6,4},{7,5},{8,10},{9,11},{10,... | collective-permute-start | bytes 737288 | tf_op jit(solution)/shard_map/ppermute | solution.py:510
  65.7 15.2 %collective-permute-start.30 = (s32[2,2,24,640]{3,2,1,0:T(8,128)S(1)}, s32[2,2,24,640]{3,2,1,0:T(8,128)S(1)}, u32[]{:S(2)}, u32[]{:S(2)}) collective-permute-start(s32[2,2,24,640]{3,2,1,0:T(8,128)S(1)} %get-tuple-element.82), channel_id=1, source_target_pairs={{0,8},{1,9},{2,4},{3,5},{4,2},{5,3},{6,14},{7,15},{8,0},{9,1},{10,... | collective-permute-start | bytes 737288 | tf_op jit(solution)/shard_map/ppermute | solution.py:510
  65.9 18.7 %collective-permute-start.28 = (s32[2,2,64,640]{3,2,1,0:T(8,128)S(1)}, s32[2,2,64,640]{3,2,1,0:T(8,128)S(1)}, u32[]{:S(2)}, u32[]{:S(2)}) collective-permute-start(s32[2,2,64,640]{3,2,1,0:T(8,128)S(1)} %get-tuple-element.80.refs_1_), channel_id=1, source_target_pairs={{0,8},{1,9},{2,10},{3,11},{4,12},{5,13},{6,14},{7,15},{8,0},{9,1},... | collective-permute-start | bytes 1966088 | tf_op jit(solution)/shard_map/ppermute | solution.py:510
  82.5 8.5 %collective-permute-start.26 = (f32[2,28,1024]{2,1,0:T(8,128)S(1)}, f32[2,28,1024]{2,1,0:T(8,128)S(1)}, u32[]{:S(2)}, u32[]{:S(2)}) collective-permute-start(f32[2,28,1024]{2,1,0:T(8,128)S(1)} %get-tuple-element.78), channel_id=1, source_target_pairs={{0,2},{1,3},{2,0},{3,1},{4,6},{5,7},{6,4},{7,5},{8,10},{9,11},{10,... | collective-permute-start | bytes 688136 | tf_op jit(solution)/shard_map/ppermute | solution.py:510
  84.6 6.5 %collective-permute-start.27 = (f32[2,28,1024]{2,1,0:T(8,128)S(1)}, f32[2,28,1024]{2,1,0:T(8,128)S(1)}, u32[]{:S(2)}, u32[]{:S(2)}) collective-permute-start(f32[2,28,1024]{2,1,0:T(8,128)S(1)} %get-tuple-element.79), channel_id=1, source_target_pairs={{0,8},{1,9},{2,4},{3,5},{4,2},{5,3},{6,14},{7,15},{8,0},{9,1},{10,... | collective-permute-start | bytes 688136 | tf_op jit(solution)/shard_map/ppermute | solution.py:510
  91.9 5.1 %collective-permute-start.33 = (f32[2,120,128]{2,1,0:T(8,128)S(1)}, f32[2,120,128]{2,1,0:T(8,128)S(1)}, u32[]{:S(2)}, u32[]{:S(2)}) collective-permute-start(f32[2,120,128]{2,1,0:T(8,128)S(1)} %get-tuple-element.86), channel_id=1, source_target_pairs={{0,1},{1,0},{2,3},{3,2},{4,5},{5,4},{6,7},{7,6},{8,9},{9,8},{10,11... | collective-permute-start | bytes 368648 | tf_op jit(solution)/shard_map/ppermute | solution.py:510
  110.6 7.2 %collective-permute-start.36 = (f32[2,28,1024]{2,1,0:T(8,128)S(1)}, f32[2,28,1024]{2,1,0:T(8,128)S(1)}, u32[]{:S(2)}, u32[]{:S(2)}) collective-permute-start(f32[2,28,1024]{2,1,0:T(8,128)S(1)} %get-tuple-element.90), channel_id=1, source_target_pairs={{0,2},{1,3},{2,0},{3,1},{4,6},{5,7},{6,4},{7,5},{8,10},{9,11},{10,... | collective-permute-start | bytes 688136 | tf_op jit(solution)/shard_map/ppermute | solution.py:510
  112.4 5.4 %collective-permute-start.37 = (f32[2,28,1024]{2,1,0:T(8,128)S(1)}, f32[2,28,1024]{2,1,0:T(8,128)S(1)}, u32[]{:S(2)}, u32[]{:S(2)}) collective-permute-start(f32[2,28,1024]{2,1,0:T(8,128)S(1)} %get-tuple-element.91), channel_id=1, source_target_pairs={{0,8},{1,9},{2,4},{3,5},{4,2},{5,3},{6,14},{7,15},{8,0},{9,1},{10,... | collective-permute-start | bytes 688136 | tf_op jit(solution)/shard_map/ppermute | solution.py:510
  118.6 4.9 %collective-permute-start.38 = (f32[2,120,128]{2,1,0:T(8,128)S(1)}, f32[2,120,128]{2,1,0:T(8,128)S(1)}, u32[]{:S(2)}, u32[]{:S(2)}) collective-permute-start(f32[2,120,128]{2,1,0:T(8,128)S(1)} %get-tuple-element.93), channel_id=1, source_target_pairs={{0,1},{1,0},{2,3},{3,2},{4,5},{5,4},{6,7},{7,6},{8,9},{9,8},{10,11... | collective-permute-start | bytes 368648 | tf_op jit(solution)/shard_map/ppermute | solution.py:510
  120.1 16.4 %collective-permute-start.12 = (f32[4,64,256]{2,1,0:T(8,128)S(1)}, f32[4,64,256]{2,1,0:T(8,128)S(1)}, u32[]{:S(2)}, u32[]{:S(2)}) collective-permute-start(f32[4,64,256]{2,1,0:T(8,128)S(1)} %get-tuple-element.63.refs_5_), channel_id=1, source_target_pairs={{0,8},{1,9},{2,10},{3,11},{4,12},{5,13},{6,14},{7,15},{8,0},{9,1},... | collective-permute-start | bytes 786440 | tf_op jit(solution)/shard_map/ppermute | solution.py:510
  120.6 15.9 %collective-permute-start.25 = (f32[4,64,256]{2,1,0:T(8,128)S(1)}, f32[4,64,256]{2,1,0:T(8,128)S(1)}, u32[]{:S(2)}, u32[]{:S(2)}) collective-permute-start(f32[4,64,256]{2,1,0:T(8,128)S(1)} %get-tuple-element.76.refs_1_), channel_id=1, source_target_pairs={{0,8},{1,9},{2,10},{3,11},{4,12},{5,13},{6,14},{7,15},{8,0},{9,1},... | collective-permute-start | bytes 786440 | tf_op jit(solution)/shard_map/ppermute | solution.py:510
  120.6 15.9 %collective-permute-start.35 = (f32[4,64,256]{2,1,0:T(8,128)S(1)}, f32[4,64,256]{2,1,0:T(8,128)S(1)}, u32[]{:S(2)}, u32[]{:S(2)}) collective-permute-start(f32[4,64,256]{2,1,0:T(8,128)S(1)} %get-tuple-element.88), channel_id=1, source_target_pairs={{0,8},{1,9},{2,10},{3,11},{4,12},{5,13},{6,14},{7,15},{8,0},{9,1},... | collective-permute-start | bytes 786440 | tf_op jit(solution)/shard_map/ppermute | solution.py:510
  138.2 5.9 %collective-permute-start.41 = (f32[4,32,256]{2,1,0:T(8,128)S(1)}, f32[4,32,256]{2,1,0:T(8,128)S(1)}, u32[]{:S(2)}, u32[]{:S(2)}) collective-permute-start(f32[4,32,256]{2,1,0:T(8,128)S(1)} %get-tuple-element.118), channel_id=1, source_target_pairs={{0,16},{1,17},{2,18},{3,19},{4,20},{5,21},{6,22},{7,23},{8,24},{9,... | collective-permute-start | bytes 393224 | tf_op jit(solution)/shard_map/ppermute | solution.py:510
  140.3 8.2 %collective-permute-start.43 = (f32[4,32,256]{2,1,0:T(8,128)S(1)}, f32[4,32,256]{2,1,0:T(8,128)S(1)}, u32[]{:S(2)}, u32[]{:S(2)}) collective-permute-start(f32[4,32,256]{2,1,0:T(8,128)S(1)} %get-tuple-element.117), channel_id=1, source_target_pairs={{0,17},{1,16},{2,19},{3,18},{4,21},{5,20},{6,23},{7,22},{8,25},{9,... | collective-permute-start | bytes 393224 | tf_op jit(solution)/shard_map/ppermute | solution.py:510
  141.8 8.1 %collective-permute-start.42 = (f32[4,32,256]{2,1,0:T(8,128)S(1)}, f32[4,32,256]{2,1,0:T(8,128)S(1)}, u32[]{:S(2)}, u32[]{:S(2)}) collective-permute-start(f32[4,32,256]{2,1,0:T(8,128)S(1)} %constant_dynamic-slice_fusion.1), channel_id=1, source_target_pairs={{0,1},{1,0},{2,3},{3,2},{4,5},{5,4},{6,7},{7,6},{8,9},{9,8},{10,11... | collective-permute-start | bytes 393224 | tf_op jit(solution)/shard_map/ppermute | solution.py:510
  (18 other events, 60.2 us)
